TPU v7x, 512 devices: a whole 4x8x8 slice. The times are simulated.
512 devices in a mesh: prompt: 2 (over y_lo), seq: 32 (over x, z), resp: 8 (over y_hi, core).
Axes of the slice: x: 4, y: 8 (y_hi: 4, y_lo: 2; y = y_hi * 2 + y_lo), z: 8, core: 2. Of those that a mesh axis runs over, the one named last changes fastest.
Arguments:
- prompt_queries: bfloat16 [8192, 8192], P(('prompt', 'seq', 'resp')), parts along dimension 0, may hold values from -20 to 20
- prompt_keys: bfloat16 [8192, 1024], P(('prompt', 'seq', 'resp')), parts along dimension 0, may hold values from -20 to 20
- prompt_values: bfloat16 [8192, 1024], P(('prompt', 'seq', 'resp')), parts along dimension 0, may hold values from -6 to 6
- answer_queries: bfloat16 [16384, 8192], P(('prompt', 'seq', 'resp')), parts along dimension 0, may hold values from -20 to 20
- answer_keys: bfloat16 [16384, 1024], P(('prompt', 'seq', 'resp')), parts along dimension 0, may hold values from -20 to 20
- answer_values: bfloat16 [16384, 1024], P(('prompt', 'seq', 'resp')), parts along dimension 0, may hold values from -6 to 6
- answer_lengths: int32 [32], P('prompt'), parts along dimension 0, may hold values from 1 to 512, 6144 in all
Outputs:
- prompt_attended: bfloat16 [8192, 8192], P(('prompt', 'seq', 'resp')), parts along dimension 0
- answer_attended: bfloat16 [16384, 8192], P(('prompt', 'seq', 'resp')), parts along dimension 0
There are 2 independent parts, one for each index of `prompt`. A program takes and returns all parts, laid end to end along the dimension named above; each array names one. Nothing has to cross between parts.
Inputs may be any that keep to these rules, and one draw needn't show every extreme that they name: `answer_lengths`: the lengths sum to 6144 and the longest is exactly 512.
All inputs are finite; a program needn't handle non-finite values.
Results may differ from a plain program's by a relative error of at most 0.008.
Values may be sent and summed in bfloat16 or wider, within the bound.
A program may use at most 64 MiB of HBM per device.

v0:
```python
import math

import jax
import jax.numpy as jnp
from jax import lax
from jax.sharding import PartitionSpec as P

DH = 128


def passed_along(value, axis, steps):
    count = lax.axis_size(axis)
    first, last = (max(0, -steps), min(count, count - steps))
    return lax.ppermute(value, axis, [(source, source + steps) for source in range(first, last)])


def online_update(state_in, queries, keys_block, values_block, allowed, score_scale):
    block_len = keys_block.shape[0]
    key_heads = queries.shape[1]
    keys_three = keys_block.reshape(block_len, key_heads, DH)
    values_three = values_block.reshape(block_len, key_heads, DH)
    scores = (
        jnp.einsum("rkgd,skd->rkgs", queries, keys_three, preferred_element_type=jnp.float32)
        * score_scale
    )
    if allowed is not None:
        scores = jnp.where(allowed[:, None, None, :], scores, -jnp.inf)
    top_old, total_old, accum_old = state_in
    top_new = jnp.maximum(top_old, jnp.max(scores, axis=-1))
    settled = jnp.where(jnp.isfinite(top_new), top_new, 0.0)
    rescale = jnp.exp(top_old - settled)
    weights = jnp.exp(scores - settled[..., None])
    total_new = total_old * rescale + jnp.sum(weights, axis=-1)
    accum_new = accum_old * rescale[..., None] + jnp.einsum(
        "rkgs,skd->rkgd",
        weights.astype(jnp.bfloat16),
        values_three,
        preferred_element_type=jnp.float32,
    )
    return (top_new, total_new, accum_new)


def blockwise(update, state_in, keys_piece, values_piece):
    length = keys_piece.shape[0]
    block_rows = math.gcd(length, 512)
    blocks = length // block_rows

    def step_once(state, inputs):
        block_keys, block_values, offset = inputs
        return (update(state, block_keys, block_values, offset), None)

    offsets = jnp.arange(blocks, dtype=jnp.int32) * block_rows
    stacked_keys = keys_piece.reshape(blocks, block_rows, keys_piece.shape[1])
    stacked_values = values_piece.reshape(blocks, block_rows, values_piece.shape[1])
    result, ignored = lax.scan(step_once, state_in, (stacked_keys, stacked_values, offsets))
    return result


def empty_state(height, key_heads, group_size):
    return (
        jnp.full((height, key_heads, group_size), -jnp.inf, jnp.float32),
        jnp.zeros((height, key_heads, group_size), jnp.float32),
        jnp.zeros((height, key_heads, group_size, DH), jnp.float32),
    )


def finish(state):
    top_score, totals, accum = state
    attended = accum / totals[..., None]
    return attended.reshape(attended.shape[0], attended.shape[1] * attended.shape[2] * DH)


def shards(
    prompt_queries,
    prompt_keys,
    prompt_values,
    answer_queries,
    answer_keys,
    answer_values,
    answer_lengths,
):
    prompt_query, prompt_key, prompt_value, answer_query, answer_key, answer_value = (
        lax.all_to_all(prompt_queries, "resp", split_axis=1, concat_axis=0, tiled=True),
        lax.all_to_all(prompt_keys, "resp", split_axis=1, concat_axis=0, tiled=True),
        lax.all_to_all(prompt_values, "resp", split_axis=1, concat_axis=0, tiled=True),
        lax.all_to_all(answer_queries, "resp", split_axis=1, concat_axis=0, tiled=True),
        lax.all_to_all(answer_keys, "resp", split_axis=1, concat_axis=0, tiled=True),
        lax.all_to_all(answer_values, "resp", split_axis=1, concat_axis=0, tiled=True),
    )
    score_scale = 1.0 / math.sqrt(DH)
    key_heads = prompt_key.shape[1] // DH
    local_heads = prompt_query.shape[1] // DH
    group_size = local_heads // key_heads
    prompt_rows = prompt_query.shape[0]
    half_rows = answer_query.shape[0]
    position = lax.axis_index("seq")
    second = position % 2
    prompt_places = position * prompt_rows + jnp.arange(prompt_rows, dtype=jnp.int32)
    answer_places = second * half_rows + jnp.arange(half_rows, dtype=jnp.int32)
    prompt_four = prompt_query.reshape(prompt_rows, key_heads, group_size, DH)
    answer_four = answer_query.reshape(half_rows, key_heads, group_size, DH)
    prior_keys, prior_values = passed_along((answer_key, answer_value), "seq", 1)
    self_keys = jnp.concatenate([prior_keys, answer_key], axis=0)
    self_values = jnp.concatenate([prior_values, answer_value], axis=0)
    self_places = jnp.concatenate([jnp.arange(half_rows, dtype=jnp.int32), answer_places])
    key_live = jnp.concatenate(
        [jnp.broadcast_to(second == 1, (half_rows,)), jnp.ones((half_rows,), bool)]
    )
    self_allowed = (self_places[None, :] <= answer_places[:, None]) & key_live[None, :]
    answer_state = online_update(
        empty_state(half_rows, key_heads, group_size),
        answer_four,
        self_keys,
        self_values,
        self_allowed,
        score_scale,
    )
    prompt_state = empty_state(prompt_rows, key_heads, group_size)

    def prompt_update(state, keys_block, values_block, offset):
        key_places = offset + jnp.arange(keys_block.shape[0], dtype=jnp.int32)
        allowed = key_places[None, :] <= prompt_places[:, None]
        return online_update(state, prompt_four, keys_block, values_block, allowed, score_scale)

    def answer_update(state, keys_block, values_block, offset):
        return online_update(state, answer_four, keys_block, values_block, None, score_scale)

    pieces = (
        lax.all_gather(prompt_key, "seq", axis=0, tiled=True),
        lax.all_gather(prompt_value, "seq", axis=0, tiled=True),
    )
    prompt_state = blockwise(prompt_update, prompt_state, pieces[0], pieces[1])
    pieces = (
        lax.all_gather(prompt_key, "seq", axis=0, tiled=True),
        lax.all_gather(prompt_value, "seq", axis=0, tiled=True),
    )
    answer_state = blockwise(answer_update, answer_state, pieces[0], pieces[1])
    prompt_result = finish(prompt_state).astype(jnp.bfloat16)
    live_length = lax.dynamic_index_in_dim(answer_lengths, position // 2, 0, keepdims=False)
    answer_result = jnp.where(
        (answer_places < live_length)[:, None], finish(answer_state), 0.0
    ).astype(jnp.bfloat16)
    return (
        lax.all_to_all(prompt_result, "resp", split_axis=0, concat_axis=1, tiled=True),
        lax.all_to_all(answer_result, "resp", split_axis=0, concat_axis=1, tiled=True),
    )


def solution(mesh):
    placed = (
        P(("prompt", "seq", "resp"), None),
        P(("prompt", "seq", "resp"), None),
        P(("prompt", "seq", "resp"), None),
        P(("prompt", "seq", "resp"), None),
        P(("prompt", "seq", "resp"), None),
        P(("prompt", "seq", "resp"), None),
        P("prompt"),
    )
    return jax.shard_map(
        shards,
        mesh=mesh,
        in_specs=placed,
        out_specs=(P(("prompt", "seq", "resp"), None), P(("prompt", "seq", "resp"), None)),
        check_vma=False,
    )
```

profile of v0, /device:TPU:1, one launch (start us, length us, event | category | flops | bytes accessed | tf_op | source)
XLA Modules:
  0.0 314.5 jit_solution(5687931987655212347)
XLA Ops:
  8.0 17.1 %all_to_all.140 = bf16[16,8,128]{2,0,1:T(8,128)(2,1)} all-to-all(bf16[16,8,128]{2,0,1:T(8,128)(2,1)S(1)} %copy_bitcast_fusion.4), channel_id=1, replica_groups=mesh['prompt'=2,'seq'=32,'resp'=8] {'resp'}, dimensions={1} | all-to-all | bytes 65536 | tf_op jit(solution)/shard_map/all_to_all | solution.py:85
  26.5 4.0 %all-to-all-start = ((bf16[16,8,128]{2,0,1:T(8,128)(2,1)}), bf16[16,8,128]{2,0,1:T(8,128)(2,1)S(1)}, u32[]{:S(2)}, u32[]{:S(2)}) async-start(bf16[16,8,128]{2,0,1:T(8,128)(2,1)} %copy_bitcast_fusion.5), calls=%async_computation | async-start | bytes 65536 | tf_op jit(solution)/shard_map/all_to_all | solution.py:84
  31.1 6.6 %all-to-all-done = bf16[16,8,128]{2,0,1:T(8,128)(2,1)S(1)} async-done(((bf16[16,8,128]{2,0,1:T(8,128)(2,1)}), bf16[16,8,128]{2,0,1:T(8,128)(2,1)S(1)}, u32[]{:S(2)}, u32[]{:S(2)}) %all-to-all-start) | async-done | bytes 32800 | tf_op jit(solution)/shard_map/all_to_all | solution.py:84
  37.7 4.0 %all-to-all-start.4 = ((bf16[32,8,128]{2,0,1:T(8,128)(2,1)}), bf16[32,8,128]{2,0,1:T(8,128)(2,1)S(1)}, u32[]{:S(2)}, u32[]{:S(2)}) async-start(bf16[32,8,128]{2,0,1:T(8,128)(2,1)} %copy_bitcast_fusion.3), calls=%async_computation.4 | async-start | bytes 131072 | tf_op jit(solution)/shard_map/all_to_all | solution.py:87
  43.2 6.0 %all-to-all-done.4 = bf16[32,8,128]{2,0,1:T(8,128)(2,1)S(1)} async-done(((bf16[32,8,128]{2,0,1:T(8,128)(2,1)}), bf16[32,8,128]{2,0,1:T(8,128)(2,1)S(1)}, u32[]{:S(2)}, u32[]{:S(2)}) %all-to-all-start.4) | async-done | bytes 65568 | tf_op jit(solution)/shard_map/all_to_all | solution.py:87
  49.2 4.0 %all-to-all-start.6 = ((bf16[32,8,128]{2,0,1:T(8,128)(2,1)}), bf16[32,8,128]{2,0,1:T(8,128)(2,1)S(1)}, u32[]{:S(2)}, u32[]{:S(2)}) async-start(bf16[32,8,128]{2,0,1:T(8,128)(2,1)} %copy_bitcast_fusion.2), calls=%async_computation.6 | async-start | bytes 131072 | tf_op jit(solution)/shard_map/all_to_all | solution.py:88
  54.9 5.8 %all-to-all-done.6 = bf16[32,8,128]{2,0,1:T(8,128)(2,1)S(1)} async-done(((bf16[32,8,128]{2,0,1:T(8,128)(2,1)}), bf16[32,8,128]{2,0,1:T(8,128)(2,1)S(1)}, u32[]{:S(2)}, u32[]{:S(2)}) %all-to-all-start.6) | async-done | bytes 65568 | tf_op jit(solution)/shard_map/all_to_all | solution.py:88
  60.7 4.1 %all-to-all-start.1 = ((bf16[16,8,1024]{2,0,1:T(8,128)(2,1)}), bf16[16,8,1024]{2,0,1:T(8,128)(2,1)S(1)}, u32[]{:S(2)}, u32[]{:S(2)}) async-start(bf16[16,8,1024]{2,0,1:T(8,128)(2,1)} %bitcast.214), calls=%async_computation.1 | async-start | bytes 524288 | tf_op jit(solution)/shard_map/all_to_all | solution.py:83
  66.7 8.8 %all-to-all-done.1 = bf16[16,8,1024]{2,0,1:T(8,128)(2,1)S(1)} async-done(((bf16[16,8,1024]{2,0,1:T(8,128)(2,1)}), bf16[16,8,1024]{2,0,1:T(8,128)(2,1)S(1)}, u32[]{:S(2)}, u32[]{:S(2)}) %all-to-all-start.1) | async-done | bytes 262176 | tf_op jit(solution)/shard_map/all_to_all | solution.py:83
  75.5 4.0 %all-to-all-start.5 = ((bf16[32,8,1024]{2,0,1:T(8,128)(2,1)}), bf16[32,8,1024]{2,0,1:T(8,128)(2,1)S(1)}, u32[]{:S(2)}, u32[]{:S(2)}) async-start(bf16[32,8,1024]{2,0,1:T(8,128)(2,1)} %bitcast.213), calls=%async_computation.5 | async-start | bytes 1048576 | tf_op jit(solution)/shard_map/all_to_all | solution.py:86
  81.8 3.8 %collective-permute-start = (bf16[256,128]{1,0:T(8,128)(2,1)S(1)}, bf16[256,128]{1,0:T(8,128)(2,1)S(1)}, u32[]{:S(2)}, u32[]{:S(2)}) collective-permute-start(bf16[256,128]{1,0:T(8,128)(2,1)S(1)} %bitcast.268), channel_id=1, source_target_pairs={{0,8},{8,16},{16,24},{24,32},{32,40},{40,48},{48,56},{56,64},{64,7... | collective-permute-start | bytes 196616 | tf_op jit(solution)/shard_map/ppermute | solution.py:14
  85.7 4.0 %collective-permute-start.1 = (bf16[256,128]{0,1:T(8,128)(2,1)S(1)}, bf16[256,128]{0,1:T(8,128)(2,1)S(1)}, u32[]{:S(2)}, u32[]{:S(2)}) collective-permute-start(bf16[256,128]{0,1:T(8,128)(2,1)S(1)} %copy.85), channel_id=1, source_target_pairs={{0,8},{8,16},{16,24},{24,32},{32,40},{40,48},{48,56},{56,64},{64,7... | collective-permute-start | bytes 196616 | tf_op jit(solution)/shard_map/ppermute | solution.py:14
  89.8 5.0 %all-to-all-done.5 = bf16[32,8,1024]{2,0,1:T(8,128)(2,1)S(1)} async-done(((bf16[32,8,1024]{2,0,1:T(8,128)(2,1)}), bf16[32,8,1024]{2,0,1:T(8,128)(2,1)S(1)}, u32[]{:S(2)}, u32[]{:S(2)}) %all-to-all-start.5) | async-done | bytes 524320 | tf_op jit(solution)/shard_map/all_to_all | solution.py:86
  97.9 3.4 %all-gather.5.cloned.1.call-done = bf16[4096,128]{1,0:T(8,128)(2,1)} async-done(((bf16[128,128]{1,0:T(8,128)(2,1)}), bf16[4096,128]{1,0:T(8,128)(2,1)}) %all-gather.5.cloned.1.call-update) | async-done | bytes 1048592 | tf_op jit(solution)/shard_map/all_gather | solution.py:130
  101.3 2.3 copy.78
  103.5 80.4 %all-gather.3.cloned.1.call-done = bf16[4096,128]{1,0:T(8,128)(2,1)} async-done(((bf16[128,128]{1,0:T(8,128)(2,1)}), bf16[4096,128]{1,0:T(8,128)(2,1)}) %all-gather.3.cloned.1.call-update) | async-done | bytes 1048592 | tf_op jit(solution)/shard_map/all_gather | solution.py:129
  184.0 36.0 %while.29 = (s32[]{:T(128)}, f32[256,1,8]{0,2,1:T(8,128)S(1)}, f32[256,1,8]{0,2,1:T(8,128)S(1)}, f32[256,1,8,128]{0,3,2,1:T(8,128)S(1)}, bf16[8,512,128]{2,1,0:T...) while((s32[]{:T(128)}, f32[256,1,8]{0,2,1:T(8,128)S(1)}, ...), condition=%wide.region_9.10_spmd, body=%wide.region_6.9_spmd.sunk | while | flops 545802240 | bytes 15615061 | solution.py:55
  190.1 2.1 fusion.95
  194.6 2.1 fusion.95
  220.0 44.0 %while.30 = (s32[]{:T(128)}, f32[128,1,8]{0,2,1:T(8,128)S(1)}, f32[128,1,8]{0,2,1:T(8,128)S(1)}, f32[128,1,8,128]{0,3,2,1:T(8,128)}, s32[8]{0:T(128)S(1)}, /*ind...) while((s32[]{:T(128)}, f32[128,1,8]{0,2,1:T(8,128)S(1)}, ...), condition=%wide.region_3.4_spmd.clone, body=%wide.region_0.3_spmd.clone.sunk | while | flops 272577152 | bytes 8075405 | solution.py:55
  222.8 2.2 fusion.102
  228.1 2.4 fusion.102
  233.6 2.4 fusion.102
  239.2 2.4 fusion.102
  244.7 2.4 fusion.102
  250.2 2.4 fusion.102
  255.7 2.4 fusion.102
  261.3 2.4 fusion.102
  266.1 11.8 %all-to-all-start.3 = ((bf16[8,16,1024]{2,1,0:T(8,128)(2,1)}), bf16[8,16,1024]{2,1,0:T(8,128)(2,1)S(1)}, u32[]{:S(2)}, u32[]{:S(2)}) async-start(bf16[8,16,1024]{2,1,0:T(8,128)(2,1)} %convert_element_type.21), calls=%async_computation.3 | async-start | bytes 524288 | tf_op jit(solution)/shard_map/all_to_all | solution.py:144
  279.6 9.1 %all-to-all-done.3 = bf16[8,16,1024]{2,1,0:T(8,128)(2,1)S(1)} async-done(((bf16[8,16,1024]{2,1,0:T(8,128)(2,1)}), bf16[8,16,1024]{2,1,0:T(8,128)(2,1)S(1)}, u32[]{:S(2)}, u32[]{:S(2)}) %all-to-all-start.3) | async-done | bytes 262176 | tf_op jit(solution)/shard_map/all_to_all | solution.py:144
  288.7 4.7 %all-to-all-start.7 = ((bf16[8,32,1024]{2,1,0:T(8,128)(2,1)}), bf16[8,32,1024]{2,1,0:T(8,128)(2,1)S(1)}, u32[]{:S(2)}, u32[]{:S(2)}) async-start(bf16[8,32,1024]{2,1,0:T(8,128)(2,1)} %select_convert_fusion), calls=%async_computation.7 | async-start | bytes 1048576 | tf_op jit(solution)/shard_map/all_to_all | solution.py:145
  294.1 12.7 %all-to-all-done.7 = bf16[8,32,1024]{2,1,0:T(8,128)(2,1)S(1)} async-done(((bf16[8,32,1024]{2,1,0:T(8,128)(2,1)}), bf16[8,32,1024]{2,1,0:T(8,128)(2,1)S(1)}, u32[]{:S(2)}, u32[]{:S(2)}) %all-to-all-start.7) | async-done | bytes 524320 | tf_op jit(solution)/shard_map/all_to_all | solution.py:145
  (181 shorter events, 74.1 us)
Async XLA Ops:
  7.2 23.3 %copy-start = (bf16[32,1024]{1,0:T(8,128)(2,1)S(1)}, bf16[32,1024]{1,0:T(8,128)(2,1)}, u32[]{:S(2)}) copy-start(bf16[32,1024]{1,0:T(8,128)(2,1)} %param.15) | copy-start | bytes 196612
  7.2 94.1 %all-gather.5.cloned.1.call-start = ((), (), s32[]{:S(2)}) async-start(), calls=%async_computation.9 | async-start | bytes 1081344 | tf_op jit(solution)/shard_map/all_gather | solution.py:130
  26.5 11.2 %all-to-all-start = ((bf16[16,8,128]{2,0,1:T(8,128)(2,1)}), bf16[16,8,128]{2,0,1:T(8,128)(2,1)S(1)}, u32[]{:S(2)}, u32[]{:S(2)}) async-start(bf16[16,8,128]{2,0,1:T(8,128)(2,1)} %copy_bitcast_fusion.5), calls=%async_computation | async-start | bytes 65536 | tf_op jit(solution)/shard_map/all_to_all | solution.py:84
  37.7 43.1 %copy-start.1 = (bf16[16,8,128]{2,0,1:T(8,128)(2,1)}, bf16[16,8,128]{2,0,1:T(8,128)(2,1)S(1)}, u32[]{:S(2)}) copy-start(bf16[16,8,128]{2,0,1:T(8,128)(2,1)S(1)} %all-to-all-done) | copy-start | bytes 98308
  37.7 11.5 %all-to-all-start.4 = ((bf16[32,8,128]{2,0,1:T(8,128)(2,1)}), bf16[32,8,128]{2,0,1:T(8,128)(2,1)S(1)}, u32[]{:S(2)}, u32[]{:S(2)}) async-start(bf16[32,8,128]{2,0,1:T(8,128)(2,1)} %copy_bitcast_fusion.3), calls=%async_computation.4 | async-start | bytes 131072 | tf_op jit(solution)/shard_map/all_to_all | solution.py:87
  49.2 11.5 %all-to-all-start.6 = ((bf16[32,8,128]{2,0,1:T(8,128)(2,1)}), bf16[32,8,128]{2,0,1:T(8,128)(2,1)S(1)}, u32[]{:S(2)}, u32[]{:S(2)}) async-start(bf16[32,8,128]{2,0,1:T(8,128)(2,1)} %copy_bitcast_fusion.2), calls=%async_computation.6 | async-start | bytes 131072 | tf_op jit(solution)/shard_map/all_to_all | solution.py:88
  60.7 14.8 %all-to-all-start.1 = ((bf16[16,8,1024]{2,0,1:T(8,128)(2,1)}), bf16[16,8,1024]{2,0,1:T(8,128)(2,1)S(1)}, u32[]{:S(2)}, u32[]{:S(2)}) async-start(bf16[16,8,1024]{2,0,1:T(8,128)(2,1)} %bitcast.214), calls=%async_computation.1 | async-start | bytes 524288 | tf_op jit(solution)/shard_map/all_to_all | solution.py:83
  75.5 19.3 %all-to-all-start.5 = ((bf16[32,8,1024]{2,0,1:T(8,128)(2,1)}), bf16[32,8,1024]{2,0,1:T(8,128)(2,1)S(1)}, u32[]{:S(2)}, u32[]{:S(2)}) async-start(bf16[32,8,1024]{2,0,1:T(8,128)(2,1)} %bitcast.213), calls=%async_computation.5 | async-start | bytes 1048576 | tf_op jit(solution)/shard_map/all_to_all | solution.py:86
  79.5 104.4 %all-gather.3.cloned.1.call-start = ((), (), s32[]{:S(2)}) async-start(), calls=%async_computation.8 | async-start | bytes 1081344 | tf_op jit(solution)/shard_map/all_gather | solution.py:129
  81.8 13.1 %collective-permute-start = (bf16[256,128]{1,0:T(8,128)(2,1)S(1)}, bf16[256,128]{1,0:T(8,128)(2,1)S(1)}, u32[]{:S(2)}, u32[]{:S(2)}) collective-permute-start(bf16[256,128]{1,0:T(8,128)(2,1)S(1)} %bitcast.268), channel_id=1, source_target_pairs={{0,8},{8,16},{16,24},{24,32},{32,40},{40,48},{48,56},{56,64},{64,7... | collective-permute-start | bytes 196616 | tf_op jit(solution)/shard_map/ppermute | solution.py:14
  85.7 11.0 %collective-permute-start.1 = (bf16[256,128]{0,1:T(8,128)(2,1)S(1)}, bf16[256,128]{0,1:T(8,128)(2,1)S(1)}, u32[]{:S(2)}, u32[]{:S(2)}) collective-permute-start(bf16[256,128]{0,1:T(8,128)(2,1)S(1)} %copy.85), channel_id=1, source_target_pairs={{0,8},{8,16},{16,24},{24,32},{32,40},{40,48},{48,56},{56,64},{64,7... | collective-permute-start | bytes 196616 | tf_op jit(solution)/shard_map/ppermute | solution.py:14
  266.1 22.5 %all-to-all-start.3 = ((bf16[8,16,1024]{2,1,0:T(8,128)(2,1)}), bf16[8,16,1024]{2,1,0:T(8,128)(2,1)S(1)}, u32[]{:S(2)}, u32[]{:S(2)}) async-start(bf16[8,16,1024]{2,1,0:T(8,128)(2,1)} %convert_element_type.21), calls=%async_computation.3 | async-start | bytes 524288 | tf_op jit(solution)/shard_map/all_to_all | solution.py:144
  288.7 18.1 %all-to-all-start.7 = ((bf16[8,32,1024]{2,1,0:T(8,128)(2,1)}), bf16[8,32,1024]{2,1,0:T(8,128)(2,1)S(1)}, u32[]{:S(2)}, u32[]{:S(2)}) async-start(bf16[8,32,1024]{2,1,0:T(8,128)(2,1)} %select_convert_fusion), calls=%async_computation.7 | async-start | bytes 1048576 | tf_op jit(solution)/shard_map/all_to_all | solution.py:145
Sparse Core Ops, SparseCore 0:
  25.3 75.9 all-gather.4
  104.4 79.4 all-gather.2
where the time goes:
time: 319 us; the launch traced here: 314 us
  waiting for transfers between devices  138 us (43%)
  matrix products  61.5 us (19%)
  starting transfers between devices  44.5 us (14%)
  local copies, waits for them, and re-layouts  19.8 us (6%)
  other arithmetic  18.3 us (6%)
  blocking collectives  17.1 us (5%)
  between operations  14.3 us (4%)
    all_gather x1, waiting for transfers between devices, shards(): lax.all_gather(prompt_key, 'seq', axis=0, tiled=True)  80.4 us
    dot_general x17, matrix products, online_update(): jnp.einsum('rkgs,skd->rkgd', weights.astype(jnp.bfloat16), values_three,...  37 us
    dot_general x17, matrix products, online_update(): jnp.einsum('rkgd,skd->rkgs', queries, keys_three, preferred_element_type=...  24.5 us
    all_to_all x1, blocking collectives, shards(): lax.all_to_all(prompt_values, 'resp', split_axis=1, concat_axis=0, tiled=...  17.1 us
    all_to_all x1, waiting for transfers between devices, shards(): lax.all_to_all(answer_result, 'resp', split_axis=0, concat_axis=1, tiled=...  12.7 us
    all_to_all x1, starting transfers between devices, shards(): lax.all_to_all(prompt_result, 'resp', split_axis=0, concat_axis=1, tiled=...  11.8 us
    all_to_all x1, waiting for transfers between devices, shards(): lax.all_to_all(prompt_result, 'resp', split_axis=0, concat_axis=1, tiled=...  9.08 us
    reduce_sum x17, other arithmetic, online_update(): total_new = total_old * rescale + jnp.sum(weights, axis=-1)  8.87 us
  transfers between devices with their start and end apart: 11, of which 9 were waited for; matrix products, arithmetic and copies ran while one was open for 5% of the time, Pallas kernels for 0%

commit v1 on v0

v1 whole, which is shorter than its diff:
```python
import math

import jax
import jax.numpy as jnp
from jax import lax
from jax.experimental import pallas as pl
from jax.experimental.pallas import tpu as pltpu
from jax.sharding import PartitionSpec as P

DH = 128
ZN = 8
SCALE = math.log2(math.e) / math.sqrt(DH)
BIG_NEG = -1e30
MESH = pl.DeviceIdType.MESH

(R_KV, R_AKV, R_QP, R_QA, R_X, R_OP, R_OA, R_KZL, R_KZR, R_KZ2, R_KYL, R_KYR, R_KY2,
 R_VYL, R_VYR, R_VY2, R_VZL, R_VZR, R_VZ2, R_AL, R_AR, R_A2) = range(22)
N_RECV = 22
N_SEND = 80


def dot_t(a, b):
    return lax.dot_general(a, b, (((1,), (1,)), ((), ())), preferred_element_type=jnp.float32)


def attend(q, pieces, state):
    scores = []
    for keys, values, mask in pieces:
        s = dot_t(q, keys())
        if mask is not None:
            s = jnp.where(mask, s, BIG_NEG)
        scores.append(s)
    top = None
    for s in scores:
        t = jnp.max(s, axis=1, keepdims=True)
        top = t if top is None else jnp.maximum(top, t)
    if state is not None:
        old_top, old_total, old_sum = state
        top = jnp.maximum(top, old_top)
    total, acc = None, None
    for s, (keys, values, mask) in zip(scores, pieces):
        p = jnp.exp2((s - top) * SCALE)
        row = jnp.sum(p, axis=1, keepdims=True)
        part = jnp.dot(p.astype(jnp.bfloat16), values(), preferred_element_type=jnp.float32)
        total = row if total is None else total + row
        acc = part if acc is None else acc + part
    if state is not None:
        rescale = jnp.exp2((old_top - top) * SCALE)
        total = total + old_total * rescale
        acc = acc + old_sum * rescale
    return top, total, acc


def kernel(pq, pk, pv, aq, ak, av, po, ao, kv, akv, qp, qa, op, oa, accs, tops, totals,
           send_sems, pout_sems, aout_sems, recv_sems):
    part = lax.axis_index("prompt")
    seq = lax.axis_index("seq")
    resp = lax.axis_index("resp")
    x, z = seq // ZN, seq % ZN
    y, core = resp // 2, resp % 2
    xb = x // 2
    xp = xb * (3 - x) + (1 - xb) * x
    zh, zb = z // 2, z % 2
    me = xb * 4 + zb * 2 + core

    def place(xx, zz, yy, cc):
        return (part, xx * ZN + zz, yy * 2 + cc)

    def member(dx, dz, dc):
        xb2, zb2, c2 = (xb + dx) % 2, (zb + dz) % 2, (core + dc) % 2
        x2 = xb2 * (3 - xp) + (1 - xb2) * xp
        return xb2 * 4 + zb2 * 2 + c2, place(x2, zh * 2 + zb2, y, c2)

    def around(v, d):
        return (v + d + 4) % 4

    def z_dev(d):
        return place(x, around(zh, d) * 2 + zb, y, core)

    def y_dev(d):
        return place(x, z, around(y, d), core)

    x_dev = place(xb * (2 + xp) + (1 - xb) * (1 - xp), z, y, core)
    xq = 1 - xp

    peers = [member(d // 4, (d // 2) % 2, d % 2) for d in range(8)]
    partners = [p[1] for p in peers[1:]] + [z_dev(1), z_dev(-1), y_dev(1), y_dev(-1), x_dev]

    barrier = pltpu.get_barrier_semaphore()
    for dev in partners:
        pl.semaphore_signal(barrier, inc=1, device_id=dev, device_id_type=MESH)

    def heads(ref, h, width):
        return ref.at[:, pl.ds(pl.multiple_of(h * width, width), width)]

    rows_p = pl.ds(pl.multiple_of(core * 16, 16), 16)
    rows_a = pl.ds(pl.multiple_of(core * 32, 32), 32)
    k_land, v_land = kv.at[0, xb, xp, zh, zb, y, rows_p], kv.at[1, xb, xp, zh, zb, y, rows_p]
    ak_land, av_land = akv.at[0, xb, zb, y, rows_a], akv.at[1, xb, zb, y, rows_a]

    for src, dst, r in (
        (heads(pk, me, DH), k_land, R_KV),
        (heads(pv, me, DH), v_land, R_KV),
        (heads(ak, me, DH), ak_land, R_AKV),
        (heads(av, me, DH), av_land, R_AKV),
        (heads(pq, me, 8 * DH), qp.at[me], R_QP),
        (heads(aq, me, 8 * DH), qa.at[me], R_QA),
    ):
        pltpu.make_async_copy(src, dst, recv_sems.at[r]).start()

    pl.semaphore_wait(barrier, len(partners))

    sends = []

    def send(src, dst, r, dev):
        copy = pltpu.make_async_remote_copy(
            src_ref=src, dst_ref=dst, send_sem=send_sems.at[len(sends)],
            recv_sem=recv_sems.at[r], device_id=dev, device_id_type=MESH)
        copy.start()
        sends.append(copy)

    def pass_on(ref, r, dev):
        send(ref, ref, r, dev)

    def arrived(ref, r):
        pltpu.make_async_copy(ref, ref, recv_sems.at[r]).wait()

    order = (7, 6, 5, 4, 3, 2, 1)
    for d in order:
        h, dev = peers[d]
        send(heads(pk, h, DH), k_land, R_KV, dev)
        send(heads(pv, h, DH), v_land, R_KV, dev)
    for d in order:
        h, dev = peers[d]
        send(heads(ak, h, DH), ak_land, R_AKV, dev)
        send(heads(av, h, DH), av_land, R_AKV, dev)

    def shard(n, dz, dy):
        return kv.at[n, :, xp, around(zh, dz), :, around(y, dy)]

    def half(n, b, dz, dy):
        return kv.at[n, b, xp, around(zh, dz), :, around(y, dy)]

    def k_plane(dy):
        return kv.at[0, :, xp, :, :, around(y, dy)]

    def v_plane(dz):
        return kv.at[1, :, xp, around(zh, dz)]

    arrived(kv.at[:, :, xp, zh, :, y], R_KV)
    pass_on(shard(0, 0, 0), R_KZL, z_dev(1))
    pass_on(shard(0, 0, 0), R_KZR, z_dev(-1))
    pass_on(shard(1, 0, 0), R_VYL, y_dev(1))
    pass_on(shard(1, 0, 0), R_VYR, y_dev(-1))
    pass_on(shard(0, 0, 0), R_X, x_dev)
    pass_on(shard(1, 0, 0), R_X, x_dev)
    for d in order:
        h, dev = peers[d]
        send(heads(pq, h, 8 * DH), qp.at[me], R_QP, dev)
    for d in order:
        h, dev = peers[d]
        send(heads(aq, h, 8 * DH), qa.at[me], R_QA, dev)
    arrived(shard(0, -1, 0), R_KZL)
    pass_on(half(0, 0, -1, 0), R_KZ2, z_dev(1))
    arrived(shard(0, 1, 0), R_KZR)
    pass_on(half(0, 1, 1, 0), R_KZ2, z_dev(-1))
    arrived(shard(1, 0, -1), R_VYL)
    pass_on(half(1, 0, 0, -1), R_VY2, y_dev(1))
    arrived(shard(1, 0, 1), R_VYR)
    pass_on(half(1, 1, 0, 1), R_VY2, y_dev(-1))
    pass_on(shard(0, -1, 0), R_X, x_dev)
    pass_on(shard(0, 1, 0), R_X, x_dev)
    pass_on(shard(1, 0, -1), R_X, x_dev)
    pass_on(shard(1, 0, 1), R_X, x_dev)
    arrived(shard(0, 2, 0), R_KZ2)
    pass_on(k_plane(0), R_KYL, y_dev(1))
    pass_on(k_plane(0), R_KYR, y_dev(-1))
    arrived(shard(1, 0, 2), R_VY2)
    pass_on(v_plane(0), R_VZL, z_dev(1))
    pass_on(v_plane(0), R_VZR, z_dev(-1))
    pass_on(shard(0, 2, 0), R_X, x_dev)
    pass_on(shard(1, 0, 2), R_X, x_dev)
    arrived(akv.at[:, :, :, y], R_AKV)
    pass_on(akv.at[:, :, :, y], R_AL, y_dev(1))
    pass_on(akv.at[:, :, :, y], R_AR, y_dev(-1))
    arrived(k_plane(-1), R_KYL)
    pass_on(kv.at[0, 0, xp, :, :, around(y, -1)], R_KY2, y_dev(1))
    arrived(k_plane(1), R_KYR)
    pass_on(kv.at[0, 1, xp, :, :, around(y, 1)], R_KY2, y_dev(-1))
    arrived(v_plane(-1), R_VZL)
    pass_on(kv.at[1, 0, xp, around(zh, -1)], R_VZ2, z_dev(1))
    arrived(v_plane(1), R_VZR)
    pass_on(kv.at[1, 1, xp, around(zh, 1)], R_VZ2, z_dev(-1))
    pass_on(k_plane(-1), R_X, x_dev)
    pass_on(v_plane(-1), R_X, x_dev)
    pass_on(k_plane(1), R_X, x_dev)
    pass_on(v_plane(1), R_X, x_dev)
    arrived(akv.at[:, :, :, around(y, -1)], R_AL)
    pass_on(akv.at[0, :, :, around(y, -1)], R_A2, y_dev(1))
    arrived(akv.at[:, :, :, around(y, 1)], R_AR)
    pass_on(akv.at[1, :, :, around(y, 1)], R_A2, y_dev(-1))
    arrived(k_plane(2), R_KY2)
    pass_on(k_plane(2), R_X, x_dev)
    arrived(v_plane(2), R_VZ2)
    pass_on(v_plane(2), R_X, x_dev)

    def piece(b, xx, mask=None):
        return (
            lambda: kv[0, b, xx].reshape(1024, DH),
            lambda: kv[1, b, xx].reshape(1024, DH),
            mask,
        )

    def row_places(base, width):
        rows = lax.broadcasted_iota(jnp.int32, (256, width), 0)
        return (rows & 31) + base

    def key_places(width):
        return lax.broadcasted_iota(jnp.int32, (256, width), 1)

    def prompt_tile(t):
        cols = [slice(j * DH, (j + 1) * DH) for j in range(8)]
        return jnp.concatenate([qp[2 * t + c, :, s] for s in cols for c in range(2)], axis=0)

    def answer_tile(m):
        return jnp.concatenate([qa[m, :, j * DH:(j + 1) * DH] for j in range(8)], axis=0)

    def keep(t, state):
        top, total, acc = state
        tops[t] = jnp.broadcast_to(top, (256, DH))
        totals[t] = jnp.broadcast_to(total, (256, DH))
        accs[t] = acc

    def kept(t):
        return tops[t][:, :1], totals[t][:, :1], accs[t]

    arrived(qp, R_QP)

    def diagonal(zbq):
        return key_places(1024) <= row_places((2 * zh + zbq) * 128 + y * 32, 1024)

    @pl.loop(0, 2)
    def _(zbq):
        keep(8 + zbq, attend(prompt_tile(zbq), [piece(0, xp, diagonal(zbq))], None))
        keep(10 + zbq, attend(
            prompt_tile(2 + zbq), [piece(0, xp), piece(1, xp, diagonal(zbq))], None))

    arrived(qa, R_QA)

    @pl.loop(0, 8)
    def _(m):
        keep(m, attend(answer_tile(m), [piece(0, xp), piece(1, xp)], None))

    arrived(kv.at[:, :, xq], R_X)

    @pl.loop(0, 4)
    def _(u):
        zbq, v = u % 2, u // 2
        t = 2 * ((1 - xp) + xp * v) + zbq
        b = (1 - xp) * v
        keep(8 + t, attend(prompt_tile(t), [piece(b, xq)], kept(8 + t)))

    arrived(akv.at[:, :, :, around(y, 2)], R_A2)

    def pout(i, j):
        dx, dz = (3 - i) // 2, (3 - i) % 2
        m, dev = member(dx, dz, j)
        return m, dev

    @pl.loop(0, 4)
    def _(i):
        m0, _ignored = member((3 - i) // 2, (3 - i) % 2, 0)
        t = m0 // 2
        _top, total, acc = kept(8 + t)
        out = (acc / total).astype(jnp.bfloat16)
        for j in range(8):
            for c in range(2):
                r = j * 32 + c * 16
                op[2 * t + c, :, j * DH:(j + 1) * DH] = out[r:r + 16]
        m1, dev1 = member((3 - i) // 2, (3 - i) % 2, 1)
        pltpu.make_async_remote_copy(
            src_ref=op.at[m1], dst_ref=heads(po, me, 8 * DH), send_sem=pout_sems.at[2 * i],
            recv_sem=recv_sems.at[R_OP], device_id=dev1, device_id_type=MESH).start()

        @pl.when(i < 3)
        def _():
            m2, dev2 = member((3 - i) // 2, (3 - i) % 2, 0)
            pltpu.make_async_remote_copy(
                src_ref=op.at[m2], dst_ref=heads(po, me, 8 * DH),
                send_sem=pout_sems.at[2 * i + 1],
                recv_sem=recv_sems.at[R_OP], device_id=dev2, device_id_type=MESH).start()

        @pl.when(i == 3)
        def _():
            pltpu.make_async_copy(op.at[me], heads(po, me, 8 * DH), recv_sems.at[R_OP]).start()

    @pl.loop(0, 8)
    def _(i):
        d = 7 - i
        m, dev = member(d // 4, (d // 2) % 2, d % 2)
        a, h = m // 4, (m // 2) % 2
        mask = key_places(512) <= row_places(h * 256 + y * 64 + (m % 2) * 32, 512)
        own_piece = (
            lambda: akv[0, a].reshape(512, DH),
            lambda: akv[1, a].reshape(512, DH),
            mask,
        )
        _top, total, acc = attend(
            answer_tile(m), [piece(0, xq), piece(1, xq), own_piece], kept(m))
        out = (acc / total).astype(jnp.bfloat16)
        for j in range(8):
            oa[m, :, j * DH:(j + 1) * DH] = out[j * 32:(j + 1) * 32]

        @pl.when(i < 7)
        def _():
            pltpu.make_async_remote_copy(
                src_ref=oa.at[m], dst_ref=heads(ao, me, 8 * DH), send_sem=aout_sems.at[i],
                recv_sem=recv_sems.at[R_OA], device_id=dev, device_id_type=MESH).start()

        @pl.when(i == 7)
        def _():
            pltpu.make_async_copy(oa.at[me], heads(ao, me, 8 * DH), recv_sems.at[R_OA]).start()

    for copy in sends:
        copy.wait_send()
    for i in range(7):
        pltpu.make_async_copy(op.at[i], op.at[i], pout_sems.at[i]).wait()
        pltpu.make_async_copy(oa.at[i], oa.at[i], aout_sems.at[i]).wait()
    arrived(po, R_OP)
    arrived(ao, R_OA)


def shards(pq, pk, pv, aq, ak, av, answer_lengths):
    bf16, f32 = jnp.bfloat16, jnp.float32
    any_spec = pl.BlockSpec(memory_space=pl.ANY)
    prompt_out, answer_out = pl.pallas_call(
        kernel,
        out_shape=(
            jax.ShapeDtypeStruct(pq.shape, bf16),
            jax.ShapeDtypeStruct(aq.shape, bf16),
        ),
        in_specs=[any_spec] * 6,
        out_specs=(any_spec, any_spec),
        scratch_shapes=[
            pltpu.VMEM((2, 2, 2, 4, 2, 4, 32, DH), bf16),
            pltpu.VMEM((2, 2, 2, 4, 64, DH), bf16),
            pltpu.VMEM((8, 16, 8 * DH), bf16),
            pltpu.VMEM((8, 32, 8 * DH), bf16),
            pltpu.VMEM((8, 16, 8 * DH), bf16),
            pltpu.VMEM((8, 32, 8 * DH), bf16),
            pltpu.VMEM((12, 256, DH), f32),
            pltpu.VMEM((12, 256, DH), f32),
            pltpu.VMEM((12, 256, DH), f32),
            pltpu.SemaphoreType.DMA((N_SEND,)),
            pltpu.SemaphoreType.DMA((8,)),
            pltpu.SemaphoreType.DMA((8,)),
            pltpu.SemaphoreType.DMA((N_RECV,)),
        ],
        compiler_params=pltpu.CompilerParams(
            collective_id=0, has_side_effects=True, vmem_limit_bytes=48 * 1024 * 1024),
        cost_estimate=pl.CostEstimate(
            flops=6_400_000_000, bytes_accessed=2_000_000, transcendentals=12_000_000),
    )(pq, pk, pv, aq, ak, av)
    seq, resp = lax.axis_index("seq"), lax.axis_index("resp")
    height = aq.shape[0]
    places = (seq % 2) * 256 + resp * height + jnp.arange(height, dtype=jnp.int32)
    live = lax.dynamic_index_in_dim(answer_lengths, seq // 2, 0, keepdims=False)
    answer_out = jnp.where((places < live)[:, None], answer_out, jnp.zeros((), bf16))
    return prompt_out, answer_out


def solution(mesh):
    rows = P(("prompt", "seq", "resp"), None)
    return jax.shard_map(
        shards,
        mesh=mesh,
        in_specs=(rows,) * 6 + (P("prompt"),),
        out_specs=(rows, rows),
        check_vma=False,
    )
```

time: 319 us -> 86 us (0.27); the launches traced: 314 us -> 85.6 us
  waiting for transfers between devices: 138 us -> 0 us
  Pallas kernels: 0 us -> 77 us
  matrix products: 61.5 us -> 0 us
  starting transfers between devices: 44.5 us -> 0 us
  blocking collectives: 17.1 us -> 0 us
  other arithmetic: 18.3 us -> 1.55 us
  between operations: 14.3 us -> 0.7 us
  local copies, waits for them, and re-layouts: 19.8 us -> 6.29 us
    all_gather x2 -> x0, waiting for transfers between devices: 83.8 us -> none  [the longest x1 80.4 us: shards(): lax.all_gather(prompt_key, 'seq', axis=0, tiled=True)]
    pallas_call x0 -> x1, Pallas kernels: none -> 77 us  [shards(): pl.pallas_call(kernel, out_shape=(jax.ShapeDtypeStruct(pq.shape, bf16), j...]
    dot_general x34 -> x0, matrix products: 61.5 us -> none  [the longest x17 37 us: online_update(): jnp.einsum('rkgs,skd->rkgd', weights.astype(jnp.bfloat16), values_three,...]
    all_to_all x7 -> x0, waiting for transfers between devices: 54 us -> none  [the longest x1 12.7 us: shards(): lax.all_to_all(answer_result, 'resp', split_axis=0, concat_axis=1, tiled=...]
    all_to_all x7 -> x0, starting transfers between devices: 36.7 us -> none  [the longest x1 11.8 us: shards(): lax.all_to_all(prompt_result, 'resp', split_axis=0, concat_axis=1, tiled=...]
    all_to_all x1 -> x0, blocking collectives: 17.1 us -> none  [shards(): lax.all_to_all(prompt_values, 'resp', split_axis=1, concat_axis=0, tiled=...]
    all_to_all x9 -> x0, local copies, waits for them, and re-layouts: 9.51 us -> none  [the longest x1 1.92 us: shards(): lax.all_to_all(answer_queries, 'resp', split_axis=1, concat_axis=0, tiled...]
    reduce_sum x17 -> x0, other arithmetic: 8.87 us -> none  [online_update(): total_new = total_old * rescale + jnp.sum(weights, axis=-1)]
  transfers between devices with their start and end apart: 11 -> 0, of which waited for: 9 -> 0; matrix products, arithmetic and copies ran while one was open for 5% -> 0% of each run, Pallas kernels for 0% -> 0%
where the time goes in v1:
time: 86 us; the launch traced here: 85.6 us
  Pallas kernels  77 us (90%)
  local copies, waits for them, and re-layouts  6.29 us (7%)
  other arithmetic  1.55 us (2%)
    pallas_call x1, Pallas kernels, shards(): pl.pallas_call(kernel, out_shape=(jax.ShapeDtypeStruct(pq.shape, bf16), j...  77 us
    unnamed x13, local copies, waits for them, and re-layouts  5.05 us

profile of v1, /device:TPU:1, one launch (start us, length us, event | category | flops | bytes accessed | tf_op | source)
XLA Modules:
  0.0 85.6 jit_solution(10811545534893437406)
XLA Ops:
  0.6 0.0 copy-start.2
  0.7 1.2 %dynamic_slice.4 = s32[1]{0:T(128)} dynamic-slice(s32[16]{0:T(128)} %param.13, s32[]{:T(128)S(6)} %select_n.21), dynamic_slice_sizes={1} | dynamic-slice | bytes 12 | tf_op jit(solution)/shard_map/jit(dynamic_index_in_dim)/dynamic_slice | solution.py:367
  1.9 0.7 add_compare_fusion
  2.6 0.0 copy-done.2
  2.6 0.0 copy-start
  2.6 1.0 %copy-done = bf16[32,8192]{1,0:T(8,128)(2,1)S(1)} copy-done((bf16[32,8192]{1,0:T(8,128)(2,1)S(1)}, bf16[32,8192]{1,0:T(8,128)(2,1)}, u32[]{:S(2)}) %copy-start) | copy-done | bytes 524312
  3.6 0.0 copy-start.1
  3.6 0.9 %copy-done.1 = bf16[16,8192]{1,0:T(8,128)(2,1)S(1)} copy-done((bf16[16,8192]{1,0:T(8,128)(2,1)S(1)}, bf16[16,8192]{1,0:T(8,128)(2,1)}, u32[]{:S(2)}) %copy-start.1) | copy-done | bytes 262168
  4.6 0.0 copy-start.3
  4.6 0.8 copy-done.3
  5.4 0.0 copy-start.4
  5.4 0.8 copy-done.4
  6.2 0.0 copy-start.5
  6.2 0.8 copy-done.5
  6.9 77.0 %shard_map.86 = (bf16[16,8192]{1,0:T(8,128)(2,1)S(1)}, bf16[32,8192]{1,0:T(8,128)(2,1)S(1)}) custom-call(bf16[16,8192]{1,0:T(8,128)(2,1)S(1)} %copy-done.1, bf16[16,1024]{1,0:T(8,128)(2,1)S(1)} %copy-done.4, bf16[16,1024]{1,0:T(8,128)(2,1)S(1)} %copy-done.5, bf16[32,8192]{1,0:T(8,128)(2,1)S(1)} %copy-done, bf16[32,1024]{1,0:T(8,128)(2,1)S(1)} %copy-done.2, ...), custom_call_target="tpu_custom_call" | custom-call | flops 6400000000 | bytes 2000000 | tf_op jit(solution)/shard_map/pallas_call | solution.py:336
  84.0 0.9 %broadcast_select_fusion = bf16[32,8192]{1,0:T(8,128)(2,1)} fusion(bf16[32,8192]{1,0:T(8,128)(2,1)S(1)} %get-tuple-element.5, pred[32]{0:T(512)(128)(4,1)S(1)} %add_compare_fusion), kind=kLoop, calls=%fused_computation | loop fusion | flops 262144 | bytes 1048608 | tf_op jit(solution)/shard_map/jit(_where)/select_n | solution.py:368
  84.9 0.7 copy.10
Async XLA Ops:
  0.6 1.9 %copy-start.2 = (bf16[32,1024]{1,0:T(8,128)(2,1)S(1)}, bf16[32,1024]{1,0:T(8,128)(2,1)}, u32[]{:S(2)}) copy-start(bf16[32,1024]{1,0:T(8,128)(2,1)} %ak.1) | copy-start | bytes 196612
  2.6 1.0 %copy-start = (bf16[32,8192]{1,0:T(8,128)(2,1)S(1)}, bf16[32,8192]{1,0:T(8,128)(2,1)}, u32[]{:S(2)}) copy-start(bf16[32,8192]{1,0:T(8,128)(2,1)} %aq.1) | copy-start | bytes 1572868
  3.6 0.9 %copy-start.1 = (bf16[16,8192]{1,0:T(8,128)(2,1)S(1)}, bf16[16,8192]{1,0:T(8,128)(2,1)}, u32[]{:S(2)}) copy-start(bf16[16,8192]{1,0:T(8,128)(2,1)} %pq.1) | copy-start | bytes 786436
  4.6 0.8 copy-start.3
  5.4 0.8 copy-start.4
  6.2 0.8 copy-start.5

commit v2 on v1

v2 whole, which is shorter than its diff:
```python
import math

import jax
import jax.numpy as jnp
from jax import lax
from jax.experimental import pallas as pl
from jax.experimental.pallas import tpu as pltpu
from jax.sharding import PartitionSpec as P

DH = 128
ZN = 8
QW = 4 * DH
SCALE = math.log2(math.e) / math.sqrt(DH)
BIG_NEG = -1e30
MESH = pl.DeviceIdType.MESH

R_KV, R_AKV, R_QP, R_QA, R_OP, R_OA, R_A = 0, 1, 2, 3, 4, 5, 6
R_FIRST, R_SECOND, R_SIB, R_ASIB = 9, 12, 24, 40
N_RECV = 44
N_SEND = 112
DISTANCES = (0, -1, 1, 2)


def dot_t(a, b):
    return lax.dot_general(a, b, (((1,), (1,)), ((), ())), preferred_element_type=jnp.float32)


def attend(q, pieces, state):
    scores = []
    for keys, values, mask in pieces:
        s = dot_t(q, keys())
        if mask is not None:
            s = jnp.where(mask, s, BIG_NEG)
        scores.append(s)
    top = None
    for s in scores:
        t = jnp.max(s, axis=1, keepdims=True)
        top = t if top is None else jnp.maximum(top, t)
    if state is not None:
        old_top, old_total, old_sum = state
        top = jnp.maximum(top, old_top)
    total, acc = None, None
    for s, (keys, values, mask) in zip(scores, pieces):
        p = jnp.exp2((s - top) * SCALE)
        row = jnp.sum(p, axis=1, keepdims=True)
        part = jnp.dot(p.astype(jnp.bfloat16), values(), preferred_element_type=jnp.float32)
        total = row if total is None else total + row
        acc = part if acc is None else acc + part
    if state is not None:
        rescale = jnp.exp2((old_top - top) * SCALE)
        total = total + old_total * rescale
        acc = acc + old_sum * rescale
    return top, total, acc


def kernel(pq, pk, pv, aq, ak, av, po, ao, kv, akv, qp, qa, op, oa, accs, tops, totals,
           send_sems, pout_sems, aout_sems, recv_sems):
    part = lax.axis_index("prompt")
    seq = lax.axis_index("seq")
    resp = lax.axis_index("resp")
    x, z = seq // ZN, seq % ZN
    y, core = resp // 2, resp % 2
    zh, zb = z // 2, z % 2
    chip = x * 2 + zb
    me = chip * 2 + core
    mine, other = x // 2, 1 - core

    def place(xx, zz, yy, cc):
        return (part, xx * ZN + zz, yy * 2 + cc)

    def chip_at(dx, dz):
        x2, zb2 = (x + dx) % 4, (zb + dz) % 2
        return x2 * 2 + zb2, x2, zh * 2 + zb2

    def around(v, d):
        return (v + d + 4) % 4

    def first(d):
        return place(x, around(zh, (1 - core) * d) * 2 + zb, around(y, core * d), core)

    def second(d):
        return place(x, around(zh, core * d) * 2 + zb, around(y, (1 - core) * d), core)

    def y_dev(d):
        return place(x, z, around(y, d), core)

    sibling = place(x, z, y, other)
    chips = [chip_at(d // 2, d % 2) for d in range(8)]
    members = [
        (h * 2 + (core + dc) % 2, place(xx, zz, y, (core + dc) % 2))
        for h, xx, zz in chips for dc in range(2)
    ]
    partners = [dev for _, dev in members[1:]] + [first(1), first(-1), second(1), second(-1)]

    barrier = pltpu.get_barrier_semaphore()
    for dev in partners:
        pl.semaphore_signal(barrier, inc=1, device_id=dev, device_id_type=MESH)

    def cut(ref, h, width):
        return ref.at[:, pl.ds(pl.multiple_of(h * width, width), width)]

    rows_p = pl.ds(pl.multiple_of(core * 16, 16), 16)
    rows_a = pl.ds(pl.multiple_of(core * 32, 32), 32)
    k_land, v_land = kv.at[0, x, zh, zb, y, rows_p], kv.at[1, x, zh, zb, y, rows_p]
    ak_land, av_land = akv.at[0, x, zb, y, rows_a], akv.at[1, x, zb, y, rows_a]

    pltpu.make_async_copy(cut(pq, me, QW), qp.at[me], recv_sems.at[R_QP]).start()
    pltpu.make_async_copy(cut(aq, me, QW), qa.at[me], recv_sems.at[R_QA]).start()
    own_parts = (
        (cut(pk, chip, DH), k_land, R_KV), (cut(pv, chip, DH), v_land, R_KV),
        (cut(ak, chip, DH), ak_land, R_AKV), (cut(av, chip, DH), av_land, R_AKV))

    @pl.when(core == mine)
    def _():
        for src, dst, r in own_parts:
            pltpu.make_async_copy(src, dst, recv_sems.at[r]).start()

    pl.semaphore_wait(barrier, len(partners))

    sends = []

    def remote(src, dst, send_sem, r, dev):
        return pltpu.make_async_remote_copy(
            src_ref=src, dst_ref=dst, send_sem=send_sem,
            recv_sem=recv_sems.at[r], device_id=dev, device_id_type=MESH)

    def send(src, dst, r, dev):
        copy = remote(src, dst, send_sems.at[len(sends)], r, dev)
        copy.start()
        sends.append(copy)

    def pass_on(ref, r, dev):
        send(ref, ref, r, dev)

    def arrived(ref, r):
        pltpu.make_async_copy(ref, ref, recv_sems.at[r]).wait()

    own_sends = [remote(src, dst, aout_sems.at[16 + i], r, sibling)
                 for i, (src, dst, r) in enumerate(own_parts)]

    def part_of(c, d1, d2, n=slice(None)):
        zz = around(zh, (1 - c) * d1 + c * d2)
        yy = around(y, (1 - c) * d2 + c * d1)
        return kv.at[n, pl.ds(2 * c, 2), zz, :, yy]

    def shard(d1, d2):
        return part_of(core, d1, d2)

    def to_sibling(d1, d2):
        k = DISTANCES.index(d2) * 4 + DISTANCES.index(d1)
        pass_on(shard(d1, d2), R_SIB + k, sibling)

    def from_sibling(d1, d2):
        k = DISTANCES.index(d2) * 4 + DISTANCES.index(d1)
        arrived(part_of(other, d1, d2), R_SIB + k)

    def start_second(d1):
        r = R_SECOND + 3 * DISTANCES.index(d1)
        pass_on(shard(d1, 0), r, second(1))
        pass_on(shard(d1, 0), r + 1, second(-1))

    def middle_second(d1):
        r = R_SECOND + 3 * DISTANCES.index(d1)
        arrived(shard(d1, -1), r)
        pass_on(part_of(core, d1, -1, 0), r + 2, second(1))
        arrived(shard(d1, 1), r + 1)
        pass_on(part_of(core, d1, 1, 1), r + 2, second(-1))
        to_sibling(d1, -1)
        to_sibling(d1, 1)

    for d in (7, 6, 5, 4, 3, 2, 1):
        h, xx, zz = chips[d]
        send(cut(pk, h, DH), k_land, R_KV, place(xx, zz, y, mine))
        send(cut(pv, h, DH), v_land, R_KV, place(xx, zz, y, mine))

    @pl.when(core != mine)
    def _():
        for copy in own_sends:
            copy.start()

    arrived(shard(0, 0), R_KV)
    pass_on(shard(0, 0), R_FIRST, first(1))
    pass_on(shard(0, 0), R_FIRST + 1, first(-1))
    start_second(0)
    to_sibling(0, 0)
    for g, dev in members[:0:-1]:
        send(cut(aq, g, QW), qa.at[me], R_QA, dev)
    arrived(shard(-1, 0), R_FIRST)
    pass_on(part_of(core, -1, 0, 0), R_FIRST + 2, first(1))
    arrived(shard(1, 0), R_FIRST + 1)
    pass_on(part_of(core, 1, 0, 1), R_FIRST + 2, first(-1))
    start_second(-1)
    start_second(1)
    to_sibling(-1, 0)
    to_sibling(1, 0)
    for d in (7, 6, 5, 4, 3, 2, 1):
        h, xx, zz = chips[d]
        send(cut(ak, h, DH), ak_land, R_AKV, place(xx, zz, y, mine))
        send(cut(av, h, DH), av_land, R_AKV, place(xx, zz, y, mine))
    middle_second(0)
    arrived(shard(2, 0), R_FIRST + 2)
    start_second(2)
    to_sibling(2, 0)
    for g, dev in members[:0:-1]:
        send(cut(pq, g, QW), qp.at[me], R_QP, dev)

    def own_keys(c, dy, n=slice(None)):
        return akv.at[n, pl.ds(2 * c, 2), :, around(y, dy)]

    arrived(own_keys(core, 0), R_AKV)
    pass_on(own_keys(core, 0), R_A, y_dev(1))
    pass_on(own_keys(core, 0), R_A + 1, y_dev(-1))
    pass_on(own_keys(core, 0), R_ASIB, sibling)
    middle_second(-1)
    middle_second(1)
    middle_second(2)
    arrived(own_keys(core, -1), R_A)
    pass_on(own_keys(core, -1, 0), R_A + 2, y_dev(1))
    arrived(own_keys(core, 1), R_A + 1)
    pass_on(own_keys(core, 1, 1), R_A + 2, y_dev(-1))
    pass_on(own_keys(core, -1), R_ASIB + 1, sibling)
    pass_on(own_keys(core, 1), R_ASIB + 2, sibling)

    def low(dy):
        def take(n):
            return kv[n, 0:2, :, :, around(y, dy)].reshape(512, DH)
        return (lambda: take(0), lambda: take(1), None)

    def high(dz):
        def take(n):
            return kv[n, 2:4, around(zh, dz)].reshape(512, DH)
        return (lambda: take(0), lambda: take(1), None)

    def slab(xx, mask=None):
        return (lambda: kv[0, xx].reshape(1024, DH), lambda: kv[1, xx].reshape(1024, DH), mask)

    def iota(width, axis):
        return lax.broadcasted_iota(jnp.int32, (256, width), axis)

    def answer_tile(t):
        return jnp.concatenate(
            [qa[2 * t + c, :, j * DH:(j + 1) * DH] for j in range(4) for c in range(2)], axis=0)

    def prompt_tile(t):
        return jnp.concatenate(
            [qp[4 * t + c, :, j * DH:(j + 1) * DH] for j in range(4) for c in range(4)], axis=0)

    def keep(t, state):
        top, total, acc = state
        tops[t] = jnp.broadcast_to(top, (256, DH))
        totals[t] = jnp.broadcast_to(total, (256, DH))
        accs[t] = acc

    def kept(t):
        return tops[t][:, :1], totals[t][:, :1], accs[t]

    for d2 in (0, -1, 1):
        for d1 in DISTANCES:
            from_sibling(d1, d2)
    arrived(qa, R_QA)

    @pl.loop(0, 8)
    def _(t):
        keep(t, attend(answer_tile(t), [f(d) for d in (0, -1, 1) for f in (low, high)], None))

    for d1 in DISTANCES:
        arrived(shard(d1, 2), R_SECOND + 3 * DISTANCES.index(d1) + 2)
        to_sibling(d1, 2)
    arrived(own_keys(core, 2), R_A + 2)
    pass_on(own_keys(core, 2), R_ASIB + 3, sibling)
    for d1 in DISTANCES:
        from_sibling(d1, 2)
    arrived(qp, R_QP)

    place_in_x = (2 * zh) * 128 + y * 32
    for t in (3, 2, 1, 0):
        rows = iota(1024, 0)
        mask = iota(1024, 1) <= place_in_x + ((rows // 32) % 2) * 128 + rows % 32
        _top, total, acc = attend(
            prompt_tile(t), [slab(i) for i in range(t)] + [slab(t, mask)], None)
        out = (acc / total).astype(jnp.bfloat16)
        for j in range(4):
            for c in range(4):
                r = j * 64 + c * 16
                op[4 * t + c, :, j * DH:(j + 1) * DH] = out[r:r + 16]
        for c in range(4):
            g = 4 * t + c
            dst = cut(po, me, QW)

            @pl.when(g != me)
            def _(g=g, c=c, dst=dst):
                remote(op.at[g], dst, pout_sems.at[g], R_OP,
                       place(t, zh * 2 + c // 2, y, c % 2)).start()

            @pl.when(g == me)
            def _(g=g, dst=dst):
                pltpu.make_async_copy(op.at[g], dst, recv_sems.at[R_OP]).start()

    for dy, r in ((0, 0), (-1, 1), (1, 2), (2, 3)):
        arrived(own_keys(other, dy), R_ASIB + r)

    @pl.loop(0, 8)
    def _(i):
        d = 7 - i
        t, xx, zz = chip_at(d // 2, d % 2)
        rows = iota(512, 0)
        mask = iota(512, 1) <= (t % 2) * 256 + y * 64 + rows % 64
        own_piece = (
            lambda: akv[0, xx].reshape(512, DH), lambda: akv[1, xx].reshape(512, DH), mask)
        _top, total, acc = attend(answer_tile(t), [low(2), high(2), own_piece], kept(t))
        out = (acc / total).astype(jnp.bfloat16)
        for j in range(4):
            for c in range(2):
                r = j * 64 + c * 32
                oa[2 * t + c, :, j * DH:(j + 1) * DH] = out[r:r + 32]
        dst = cut(ao, me, QW)
        remote(oa.at[2 * t + other], dst, aout_sems.at[i], R_OA, place(xx, zz, y, other)).start()

        @pl.when(i < 7)
        def _():
            remote(oa.at[2 * t + core], dst, aout_sems.at[8 + i], R_OA,
                   place(xx, zz, y, core)).start()

        @pl.when(i == 7)
        def _():
            pltpu.make_async_copy(oa.at[me], dst, recv_sems.at[R_OA]).start()

    assert len(sends) <= N_SEND
    for copy in sends:
        copy.wait_send()

    @pl.when(core != mine)
    def _():
        for copy in own_sends:
            copy.wait_send()

    for g in range(16):
        @pl.when(g != me)
        def _(g=g):
            pltpu.make_async_copy(op.at[g], op.at[g], pout_sems.at[g]).wait()

    for i in range(15):
        pltpu.make_async_copy(oa.at[i], oa.at[i], aout_sems.at[i]).wait()
    arrived(po, R_OP)
    arrived(ao, R_OA)


def shards(pq, pk, pv, aq, ak, av, answer_lengths):
    bf16, f32 = jnp.bfloat16, jnp.float32
    any_spec = pl.BlockSpec(memory_space=pl.ANY)
    prompt_out, answer_out = pl.pallas_call(
        kernel,
        out_shape=(
            jax.ShapeDtypeStruct(pq.shape, bf16),
            jax.ShapeDtypeStruct(aq.shape, bf16),
        ),
        in_specs=[any_spec] * 6,
        out_specs=(any_spec, any_spec),
        scratch_shapes=[
            pltpu.VMEM((2, 4, 4, 2, 4, 32, DH), bf16),
            pltpu.VMEM((2, 4, 2, 4, 64, DH), bf16),
            pltpu.VMEM((16, 16, QW), bf16),
            pltpu.VMEM((16, 32, QW), bf16),
            pltpu.VMEM((16, 16, QW), bf16),
            pltpu.VMEM((16, 32, QW), bf16),
            pltpu.VMEM((8, 256, DH), f32),
            pltpu.VMEM((8, 256, DH), f32),
            pltpu.VMEM((8, 256, DH), f32),
            pltpu.SemaphoreType.DMA((N_SEND,)),
            pltpu.SemaphoreType.DMA((16,)),
            pltpu.SemaphoreType.DMA((20,)),
            pltpu.SemaphoreType.DMA((N_RECV,)),
        ],
        compiler_params=pltpu.CompilerParams(
            collective_id=0, has_side_effects=True, vmem_limit_bytes=60 * 1024 * 1024),
        cost_estimate=pl.CostEstimate(
            flops=6_400_000_000, bytes_accessed=2_000_000, transcendentals=12_000_000),
    )(pq, pk, pv, aq, ak, av)
    seq, resp = lax.axis_index("seq"), lax.axis_index("resp")
    height = aq.shape[0]
    places = (seq % 2) * 256 + resp * height + jnp.arange(height, dtype=jnp.int32)
    live = lax.dynamic_index_in_dim(answer_lengths, seq // 2, 0, keepdims=False)
    answer_out = jnp.where((places < live)[:, None], answer_out, jnp.zeros((), bf16))
    return prompt_out, answer_out


def solution(mesh):
    rows = P(("prompt", "seq", "resp"), None)
    return jax.shard_map(
        shards,
        mesh=mesh,
        in_specs=(rows,) * 6 + (P("prompt"),),
        out_specs=(rows, rows),
        check_vma=False,
    )
```

time: 86 us -> 79.6 us (0.926)
  local copies, waits for them, and re-layouts: 6.29 us -> 1.94 us
  Pallas kernels: 77 us -> 74.2 us
  other arithmetic: 1.55 us -> 2.63 us
    unnamed x13 -> x5, local copies, waits for them, and re-layouts: 5.05 us -> 1.35 us
    pallas_call x1, Pallas kernels: 77 us -> 74.2 us  [shards(): pl.pallas_call(kernel, out_shape=(jax.ShapeDtypeStruct(pq.shape, bf16), j...]
    select_n x1, other arithmetic: 0.9 us -> 1.98 us  [shards(): jnp.where((places < live)[:, None], answer_out, jnp.zeros((), bf16))]
where the time goes in v2:
time: 79.6 us; the launch traced here: 79.4 us
  Pallas kernels  74.2 us (93%)
  other arithmetic  2.63 us (3%)
  local copies, waits for them, and re-layouts  1.94 us (2%)
    pallas_call x1, Pallas kernels, shards(): pl.pallas_call(kernel, out_shape=(jax.ShapeDtypeStruct(pq.shape, bf16), j...  74.2 us
    select_n x1, other arithmetic, shards(): jnp.where((places < live)[:, None], answer_out, jnp.zeros((), bf16))  1.98 us

profile of v2, /device:TPU:1, one launch (start us, length us, event | category | flops | bytes accessed | tf_op | source)
XLA Modules:
  0.0 79.4 jit_solution(15185123574267711947)
XLA Ops:
  0.7 0.0 copy-start.1
  0.7 0.6 copy-done.1
  1.3 0.6 dynamic_slice.4
  1.9 0.7 add_compare_fusion
  2.5 74.2 %shard_map.86 = (bf16[16,8192]{1,0:T(8,128)(2,1)}, bf16[32,8192]{1,0:T(8,128)(2,1)}) custom-call(bf16[16,8192]{1,0:T(8,128)(2,1)} %pq.1, bf16[16,1024]{1,0:T(8,128)(2,1)} %pk.1, bf16[16,1024]{1,0:T(8,128)(2,1)} %pv.1, bf16[32,8192]{1,0:T(8,128)(2,1)} %aq.1, bf16[32,1024]{1,0:T(8,128)(2,1)} %ak.1, bf16[32,1024]{1,0:T(8,128)(2,1)} %av.1), custom_call_target="tpu_custom_call" | custom-call | flops 6400000000 | bytes 2000000 | tf_op jit(solution)/shard_map/pallas_call | solution.py:351
  76.7 0.0 copy-start
  76.8 2.0 %broadcast_select_fusion = bf16[32,8192]{1,0:T(8,128)(2,1)} fusion(bf16[32,8192]{1,0:T(8,128)(2,1)} %get-tuple-element.5, pred[32]{0:T(512)(128)(4,1)S(1)} %add_compare_fusion), kind=kLoop, calls=%fused_computation | loop fusion | flops 262144 | bytes 1048608 | tf_op jit(solution)/shard_map/jit(_where)/select_n | solution.py:383
  78.7 0.0 copy-done
  78.7 0.7 copy.10
Async XLA Ops:
  0.7 0.7 copy-start.1
  76.7 2.0 %copy-start = (bf16[16,8192]{1,0:T(8,128)(2,1)S(1)}, bf16[16,8192]{1,0:T(8,128)(2,1)}, u32[]{:S(2)}) copy-start(bf16[16,8192]{1,0:T(8,128)(2,1)} %get-tuple-element.8) | copy-start | bytes 786436

commit v3 on v2

--- a/solution.py
+++ b/solution.py
@@ -25,35 +25,65 @@
     return lax.dot_general(a, b, (((1,), (1,)), ((), ())), preferred_element_type=jnp.float32)
 
 
-def attend(q, pieces, state):
-    scores = []
-    for keys, values, mask in pieces:
-        s = dot_t(q, keys())
-        if mask is not None:
-            s = jnp.where(mask, s, BIG_NEG)
-        scores.append(s)
+def fold_max(s, top):
+    for i in range(s.shape[1] // DH):
+        c = s[:, i * DH:(i + 1) * DH]
+        top = c if top is None else jnp.maximum(top, c)
+    return top
+
+
+def score_piece(item, i, top):
+    keys, _values, mask = item.pieces[i]
+    s = dot_t(item.q, keys())
+    if mask is not None:
+        s = jnp.where(mask(), s, BIG_NEG)
+    item.buffer(i)[...] = s
+    return fold_max(s, top)
+
+
+def weigh_piece(item, i, top, acc):
+    _keys, values, _mask = item.pieces[i]
+    p = jnp.exp2((item.buffer(i)[...] - top) * SCALE).astype(jnp.bfloat16)
+    v = values()
+    v = jnp.concatenate([v, jnp.ones(v.shape, v.dtype)], axis=1)
+    part = jnp.dot(p, v, preferred_element_type=jnp.float32)
+    return part if acc is None else acc + part
+
+
+def row_top(folded, old):
+    top = jnp.max(folded, axis=1, keepdims=True)
+    return top if old is None else jnp.maximum(top, old)
+
+
+class Item:
+    def __init__(self, load, pieces, buffer, state=None):
+        self.load, self.pieces, self.buffer, self.state = load, pieces, buffer, state
+
+
+def run_items(items, between):
     top = None
-    for s in scores:
-        t = jnp.max(s, axis=1, keepdims=True)
-        top = t if top is None else jnp.maximum(top, t)
-    if state is not None:
-        old_top, old_total, old_sum = state
-        top = jnp.maximum(top, old_top)
-    total, acc = None, None
-    for s, (keys, values, mask) in zip(scores, pieces):
-        p = jnp.exp2((s - top) * SCALE)
-        row = jnp.sum(p, axis=1, keepdims=True)
-        part = jnp.dot(p.astype(jnp.bfloat16), values(), preferred_element_type=jnp.float32)
-        total = row if total is None else total + row
-        acc = part if acc is None else acc + part
-    if state is not None:
-        rescale = jnp.exp2((old_top - top) * SCALE)
-        total = total + old_total * rescale
-        acc = acc + old_sum * rescale
-    return top, total, acc
-
-
-def kernel(pq, pk, pv, aq, ak, av, po, ao, kv, akv, qp, qa, op, oa, accs, tops, totals,
+    for n in range(len(items) + 1):
+        new = items[n] if n < len(items) else None
+        now = items[n - 1] if n > 0 else None
+        folded, acc = None, None
+        if new is not None:
+            new.q = new.load()
+        for i in range(max(len(v.pieces) for v in (new, now) if v is not None)):
+            if new is not None and i < len(new.pieces):
+                folded = score_piece(new, i, folded)
+            if now is not None and i < len(now.pieces):
+                acc = weigh_piece(now, i, top, acc)
+        if now is not None and now.state is not None:
+            old_top, old_acc = now.state()
+            acc = acc + old_acc * jnp.exp2((old_top - top) * SCALE)
+        now_top = top
+        if new is not None:
+            top = row_top(folded, None if new.state is None else new.state()[0])
+        if now is not None:
+            between(n - 1, now_top, acc)
+
+
+def kernel(pq, pk, pv, aq, ak, av, po, ao, kv, akv, qp, qa, op, oa, accs, tops, s0, s1,
            send_sems, pout_sems, aout_sems, recv_sems):
     part = lax.axis_index("prompt")
     seq = lax.axis_index("seq")
@@ -214,12 +244,7 @@
     middle_second(-1)
     middle_second(1)
     middle_second(2)
-    arrived(own_keys(core, -1), R_A)
-    pass_on(own_keys(core, -1, 0), R_A + 2, y_dev(1))
-    arrived(own_keys(core, 1), R_A + 1)
-    pass_on(own_keys(core, 1, 1), R_A + 2, y_dev(-1))
-    pass_on(own_keys(core, -1), R_ASIB + 1, sibling)
-    pass_on(own_keys(core, 1), R_ASIB + 2, sibling)
+    bufs = (s0, s1)
 
     def low(dy):
         def take(n):
@@ -231,99 +256,130 @@
             return kv[n, 2:4, around(zh, dz)].reshape(512, DH)
         return (lambda: take(0), lambda: take(1), None)
 
-    def slab(xx, mask=None):
-        return (lambda: kv[0, xx].reshape(1024, DH), lambda: kv[1, xx].reshape(1024, DH), mask)
-
-    def iota(width, axis):
-        return lax.broadcasted_iota(jnp.int32, (256, width), axis)
+    def half_slab(xx, h, mask=None):
+        def take(n):
+            return kv[n, xx, 2 * h:2 * h + 2].reshape(512, DH)
+        return (lambda: take(0), lambda: take(1), mask)
+
+    def iota(height, axis):
+        return lax.broadcasted_iota(jnp.int32, (height, 512), axis)
 
     def answer_tile(t):
         return jnp.concatenate(
-            [qa[2 * t + c, :, j * DH:(j + 1) * DH] for j in range(4) for c in range(2)], axis=0)
+            [qa[4 * t + c, :, j * DH:(j + 1) * DH] for j in range(4) for c in range(4)], axis=0)
 
     def prompt_tile(t):
         return jnp.concatenate(
             [qp[4 * t + c, :, j * DH:(j + 1) * DH] for j in range(4) for c in range(4)], axis=0)
 
-    def keep(t, state):
-        top, total, acc = state
-        tops[t] = jnp.broadcast_to(top, (256, DH))
-        totals[t] = jnp.broadcast_to(total, (256, DH))
-        accs[t] = acc
-
-    def kept(t):
-        return tops[t][:, :1], totals[t][:, :1], accs[t]
+    def wide(b):
+        return lambda i: bufs[b].at[i]
+
+    def tall(b):
+        return lambda i: bufs[b].at[i // 2, (i % 2) * 256:(i % 2) * 256 + 256]
 
     for d2 in (0, -1, 1):
         for d1 in DISTANCES:
             from_sibling(d1, d2)
     arrived(qa, R_QA)
 
-    @pl.loop(0, 8)
-    def _(t):
-        keep(t, attend(answer_tile(t), [f(d) for d in (0, -1, 1) for f in (low, high)], None))
-
-    for d1 in DISTANCES:
-        arrived(shard(d1, 2), R_SECOND + 3 * DISTANCES.index(d1) + 2)
-        to_sibling(d1, 2)
-    arrived(own_keys(core, 2), R_A + 2)
-    pass_on(own_keys(core, 2), R_ASIB + 3, sibling)
+    first_items = [
+        Item(lambda t=t: answer_tile(t),
+             [f(d) for d in (0, -1, 1) for f in (low, high)], wide(t % 2))
+        for t in range(4)]
+
+    def after_first(n, top, acc):
+        tops[n] = jnp.broadcast_to(top, (512, DH))
+        accs[n] = acc
+        if n == 1:
+            arrived(own_keys(core, -1), R_A)
+            pass_on(own_keys(core, -1, 0), R_A + 2, y_dev(1))
+            arrived(own_keys(core, 1), R_A + 1)
+            pass_on(own_keys(core, 1, 1), R_A + 2, y_dev(-1))
+            pass_on(own_keys(core, -1), R_ASIB + 1, sibling)
+            pass_on(own_keys(core, 1), R_ASIB + 2, sibling)
+        if n == 2:
+            for d1 in DISTANCES:
+                arrived(shard(d1, 2), R_SECOND + 3 * DISTANCES.index(d1) + 2)
+                to_sibling(d1, 2)
+
+    run_items(first_items, after_first)
+
     for d1 in DISTANCES:
         from_sibling(d1, 2)
     arrived(qp, R_QP)
-
-    place_in_x = (2 * zh) * 128 + y * 32
-    for t in (3, 2, 1, 0):
-        rows = iota(1024, 0)
-        mask = iota(1024, 1) <= place_in_x + ((rows // 32) % 2) * 128 + rows % 32
-        _top, total, acc = attend(
-            prompt_tile(t), [slab(i) for i in range(t)] + [slab(t, mask)], None)
-        out = (acc / total).astype(jnp.bfloat16)
+    arrived(own_keys(core, 2), R_A + 2)
+    pass_on(own_keys(core, 2), R_ASIB + 3, sibling)
+
+    def prompt_mask(h):
+        rows = iota(256, 0)
+        here = (2 * zh) * 128 + y * 32 + ((rows // 32) % 2) * 128 + rows % 32
+        return iota(256, 1) + h * 512 <= here
+
+    def answer_mask():
+        rows = iota(512, 0)
+        return iota(512, 1) <= ((rows // 64) % 2) * 256 + y * 64 + rows % 64
+
+    prompt_order = (3, 2, 1, 0)
+    answer_order = (2, 1, 3, 0)
+    second_items = []
+    for t in prompt_order:
+        pieces = [half_slab(i, h) for i in range(t) for h in range(2)]
+        pieces += [half_slab(t, h, lambda h=h: prompt_mask(h)) for h in range(2)]
+        second_items.append(Item(lambda t=t: prompt_tile(t), pieces, tall(len(second_items) % 2)))
+    for dx in answer_order:
+        t = (x + dx) % 4
+        own_piece = (
+            lambda t=t: akv[0, t].reshape(512, DH), lambda t=t: akv[1, t].reshape(512, DH),
+            answer_mask)
+        second_items.append(Item(
+            lambda t=t: answer_tile(t), [low(2), high(2), own_piece], wide(len(second_items) % 2),
+            lambda t=t: (tops[t][:, :1], accs[t])))
+
+    def finished(acc):
+        return (acc[:, :DH] / acc[:, DH:]).astype(jnp.bfloat16)
+
+    def after_second(n, top, acc):
+        if n < 4:
+            t = prompt_order[n]
+            out = finished(acc)
+            for j in range(4):
+                for c in range(4):
+                    r = j * 64 + c * 16
+                    op[4 * t + c, :, j * DH:(j + 1) * DH] = out[r:r + 16]
+            for c in range(4):
+                g = 4 * t + c
+                dst = cut(po, me, QW)
+
+                @pl.when(g != me)
+                def _(g=g, c=c, dst=dst):
+                    remote(op.at[g], dst, pout_sems.at[g], R_OP,
+                           place(t, zh * 2 + c // 2, y, c % 2)).start()
+
+                @pl.when(g == me)
+                def _(g=g, dst=dst):
+                    pltpu.make_async_copy(op.at[g], dst, recv_sems.at[R_OP]).start()
+            if n == 2:
+                for dy, r in ((0, 0), (-1, 1), (1, 2), (2, 3)):
+                    arrived(own_keys(other, dy), R_ASIB + r)
+            return
+        dx = answer_order[n - 4]
+        t = (x + dx) % 4
+        out = finished(acc)
         for j in range(4):
             for c in range(4):
-                r = j * 64 + c * 16
-                op[4 * t + c, :, j * DH:(j + 1) * DH] = out[r:r + 16]
-        for c in range(4):
-            g = 4 * t + c
-            dst = cut(po, me, QW)
-
-            @pl.when(g != me)
-            def _(g=g, c=c, dst=dst):
-                remote(op.at[g], dst, pout_sems.at[g], R_OP,
-                       place(t, zh * 2 + c // 2, y, c % 2)).start()
-
-            @pl.when(g == me)
-            def _(g=g, dst=dst):
-                pltpu.make_async_copy(op.at[g], dst, recv_sems.at[R_OP]).start()
-
-    for dy, r in ((0, 0), (-1, 1), (1, 2), (2, 3)):
-        arrived(own_keys(other, dy), R_ASIB + r)
-
-    @pl.loop(0, 8)
-    def _(i):
-        d = 7 - i
-        t, xx, zz = chip_at(d // 2, d % 2)
-        rows = iota(512, 0)
-        mask = iota(512, 1) <= (t % 2) * 256 + y * 64 + rows % 64
-        own_piece = (
-            lambda: akv[0, xx].reshape(512, DH), lambda: akv[1, xx].reshape(512, DH), mask)
-        _top, total, acc = attend(answer_tile(t), [low(2), high(2), own_piece], kept(t))
-        out = (acc / total).astype(jnp.bfloat16)
-        for j in range(4):
-            for c in range(2):
-                r = j * 64 + c * 32
-                oa[2 * t + c, :, j * DH:(j + 1) * DH] = out[r:r + 32]
+                r = j * 128 + c * 32
+                oa[4 * t + c, :, j * DH:(j + 1) * DH] = out[r:r + 32]
         dst = cut(ao, me, QW)
-        remote(oa.at[2 * t + other], dst, aout_sems.at[i], R_OA, place(xx, zz, y, other)).start()
-
-        @pl.when(i < 7)
-        def _():
-            remote(oa.at[2 * t + core], dst, aout_sems.at[8 + i], R_OA,
-                   place(xx, zz, y, core)).start()
-
-        @pl.when(i == 7)
-        def _():
-            pltpu.make_async_copy(oa.at[me], dst, recv_sems.at[R_OA]).start()
+        for k in (3, 2, 1, 0):
+            d = dx * 4 + k
+            g, dev = members[d]
+            if d:
+                remote(oa.at[g], dst, aout_sems.at[d], R_OA, dev).start()
+            else:
+                pltpu.make_async_copy(oa.at[g], dst, recv_sems.at[R_OA]).start()
+
+    run_items(second_items, after_second)
 
     assert len(sends) <= N_SEND
     for copy in sends:
@@ -339,7 +395,7 @@
         def _(g=g):
             pltpu.make_async_copy(op.at[g], op.at[g], pout_sems.at[g]).wait()
 
-    for i in range(15):
+    for i in range(1, 16):
         pltpu.make_async_copy(oa.at[i], oa.at[i], aout_sems.at[i]).wait()
     arrived(po, R_OP)
     arrived(ao, R_OA)
@@ -363,9 +419,10 @@
             pltpu.VMEM((16, 32, QW), bf16),
             pltpu.VMEM((16, 16, QW), bf16),
             pltpu.VMEM((16, 32, QW), bf16),
-            pltpu.VMEM((8, 256, DH), f32),
-            pltpu.VMEM((8, 256, DH), f32),
-            pltpu.VMEM((8, 256, DH), f32),
+            pltpu.VMEM((4, 512, 2 * DH), f32),
+            pltpu.VMEM((4, 512, DH), f32),
+            pltpu.VMEM((6, 512, 512), f32),
+            pltpu.VMEM((6, 512, 512), f32),
             pltpu.SemaphoreType.DMA((N_SEND,)),
             pltpu.SemaphoreType.DMA((16,)),
             pltpu.SemaphoreType.DMA((20,)),

time: 79.6 us -> 72.6 us (0.912)
  Pallas kernels: 74.2 us -> 67.2 us
    pallas_call x1, Pallas kernels: 74.2 us -> 67.2 us  [shards(): pl.pallas_call(kernel, out_shape=(jax.ShapeDtypeStruct(pq.shape, bf16), j...]
where the time goes in v3:
time: 72.6 us; the launch traced here: 72.4 us
  Pallas kernels  67.2 us (93%)
  other arithmetic  2.63 us (4%)
  local copies, waits for them, and re-layouts  1.94 us (3%)
    pallas_call x1, Pallas kernels, shards(): pl.pallas_call(kernel, out_shape=(jax.ShapeDtypeStruct(pq.shape, bf16), j...  67.2 us
    select_n x1, other arithmetic, shards(): jnp.where((places < live)[:, None], answer_out, jnp.zeros((), bf16))  1.98 us

profile of v3, /device:TPU:1, one launch (start us, length us, event | category | flops | bytes accessed | tf_op | source)
XLA Modules:
  0.0 72.4 jit_solution(5352498164234490796)
XLA Ops:
  0.7 0.0 copy-start.1
  0.7 0.6 copy-done.1
  1.3 0.6 dynamic_slice.4
  1.9 0.7 add_compare_fusion
  2.5 67.2 %shard_map.86 = (bf16[16,8192]{1,0:T(8,128)(2,1)}, bf16[32,8192]{1,0:T(8,128)(2,1)}) custom-call(bf16[16,8192]{1,0:T(8,128)(2,1)} %pq.1, bf16[16,1024]{1,0:T(8,128)(2,1)} %pk.1, bf16[16,1024]{1,0:T(8,128)(2,1)} %pv.1, bf16[32,8192]{1,0:T(8,128)(2,1)} %aq.1, bf16[32,1024]{1,0:T(8,128)(2,1)} %ak.1, bf16[32,1024]{1,0:T(8,128)(2,1)} %av.1), custom_call_target="tpu_custom_call" | custom-call | flops 6400000000 | bytes 2000000 | tf_op jit(solution)/shard_map/pallas_call | solution.py:407
  69.7 0.0 copy-start
  69.7 2.0 %broadcast_select_fusion = bf16[32,8192]{1,0:T(8,128)(2,1)} fusion(bf16[32,8192]{1,0:T(8,128)(2,1)} %get-tuple-element.5, pred[32]{0:T(512)(128)(4,1)S(1)} %add_compare_fusion), kind=kLoop, calls=%fused_computation | loop fusion | flops 262144 | bytes 1048608 | tf_op jit(solution)/shard_map/jit(_where)/select_n | solution.py:440
  71.7 0.0 copy-done
  71.7 0.7 copy.10
Async XLA Ops:
  0.7 0.7 copy-start.1
  69.7 2.0 %copy-start = (bf16[16,8192]{1,0:T(8,128)(2,1)S(1)}, bf16[16,8192]{1,0:T(8,128)(2,1)}, u32[]{:S(2)}) copy-start(bf16[16,8192]{1,0:T(8,128)(2,1)} %get-tuple-element.8) | copy-start | bytes 786436

commit v4 on v3

--- a/solution.py
+++ b/solution.py
@@ -120,7 +120,7 @@
         (h * 2 + (core + dc) % 2, place(xx, zz, y, (core + dc) % 2))
         for h, xx, zz in chips for dc in range(2)
     ]
-    partners = [dev for _, dev in members[1:]] + [first(1), first(-1), second(1), second(-1)]
+    partners = [dev for _, dev in members[1:]] + [f(d) for f in (first, second) for d in (1, -1, 2)]
 
     barrier = pltpu.get_barrier_semaphore()
     for dev in partners:
@@ -184,19 +184,19 @@
         k = DISTANCES.index(d2) * 4 + DISTANCES.index(d1)
         arrived(part_of(other, d1, d2), R_SIB + k)
 
+    def start_first():
+        for k, d in enumerate((1, -1, 2)):
+            pass_on(shard(0, 0), R_FIRST + k, first(d))
+
     def start_second(d1):
         r = R_SECOND + 3 * DISTANCES.index(d1)
-        pass_on(shard(d1, 0), r, second(1))
-        pass_on(shard(d1, 0), r + 1, second(-1))
-
-    def middle_second(d1):
-        r = R_SECOND + 3 * DISTANCES.index(d1)
-        arrived(shard(d1, -1), r)
-        pass_on(part_of(core, d1, -1, 0), r + 2, second(1))
-        arrived(shard(d1, 1), r + 1)
-        pass_on(part_of(core, d1, 1, 1), r + 2, second(-1))
-        to_sibling(d1, -1)
-        to_sibling(d1, 1)
+        for k, d in enumerate((1, -1, 2)):
+            pass_on(shard(d1, 0), r + k, second(d))
+
+    def hand_over(d1, d2):
+        k = DISTANCES[1:].index(d2)
+        arrived(shard(d1, d2), R_SECOND + 3 * DISTANCES.index(d1) + k)
+        to_sibling(d1, d2)
 
     for d in (7, 6, 5, 4, 3, 2, 1):
         h, xx, zz = chips[d]
@@ -209,41 +209,25 @@
             copy.start()
 
     arrived(shard(0, 0), R_KV)
-    pass_on(shard(0, 0), R_FIRST, first(1))
-    pass_on(shard(0, 0), R_FIRST + 1, first(-1))
+    start_first()
     start_second(0)
     to_sibling(0, 0)
     for g, dev in members[:0:-1]:
         send(cut(aq, g, QW), qa.at[me], R_QA, dev)
-    arrived(shard(-1, 0), R_FIRST)
-    pass_on(part_of(core, -1, 0, 0), R_FIRST + 2, first(1))
-    arrived(shard(1, 0), R_FIRST + 1)
-    pass_on(part_of(core, 1, 0, 1), R_FIRST + 2, first(-1))
-    start_second(-1)
-    start_second(1)
-    to_sibling(-1, 0)
-    to_sibling(1, 0)
+    for k, d1 in enumerate((-1, 1, 2)):
+        arrived(shard(d1, 0), R_FIRST + k)
+        start_second(d1)
+        to_sibling(d1, 0)
     for d in (7, 6, 5, 4, 3, 2, 1):
         h, xx, zz = chips[d]
         send(cut(ak, h, DH), ak_land, R_AKV, place(xx, zz, y, mine))
         send(cut(av, h, DH), av_land, R_AKV, place(xx, zz, y, mine))
-    middle_second(0)
-    arrived(shard(2, 0), R_FIRST + 2)
-    start_second(2)
-    to_sibling(2, 0)
     for g, dev in members[:0:-1]:
         send(cut(pq, g, QW), qp.at[me], R_QP, dev)
 
     def own_keys(c, dy, n=slice(None)):
         return akv.at[n, pl.ds(2 * c, 2), :, around(y, dy)]
 
-    arrived(own_keys(core, 0), R_AKV)
-    pass_on(own_keys(core, 0), R_A, y_dev(1))
-    pass_on(own_keys(core, 0), R_A + 1, y_dev(-1))
-    pass_on(own_keys(core, 0), R_ASIB, sibling)
-    middle_second(-1)
-    middle_second(1)
-    middle_second(2)
     bufs = (s0, s1)
 
     def low(dy):
@@ -278,19 +262,39 @@
     def tall(b):
         return lambda i: bufs[b].at[i // 2, (i % 2) * 256:(i % 2) * 256 + 256]
 
-    for d2 in (0, -1, 1):
-        for d1 in DISTANCES:
-            from_sibling(d1, d2)
-    arrived(qa, R_QA)
-
-    first_items = [
-        Item(lambda t=t: answer_tile(t),
-             [f(d) for d in (0, -1, 1) for f in (low, high)], wide(t % 2))
-        for t in range(4)]
-
-    def after_first(n, top, acc):
+    def keep(n, top, acc):
         tops[n] = jnp.broadcast_to(top, (512, DH))
         accs[n] = acc
+
+    def kept(t):
+        return tops[t][:, :1], accs[t]
+
+    for d1 in DISTANCES:
+        from_sibling(d1, 0)
+    arrived(qa, R_QA)
+
+    def after_first(n, top, acc):
+        keep(n, top, acc)
+        if n == 0:
+            arrived(own_keys(core, 0), R_AKV)
+            pass_on(own_keys(core, 0), R_A, y_dev(1))
+            pass_on(own_keys(core, 0), R_A + 1, y_dev(-1))
+            pass_on(own_keys(core, 0), R_ASIB, sibling)
+        else:
+            for d1 in ((), (0,), (-1, 1), (2,))[n]:
+                hand_over(d1, -1)
+                hand_over(d1, 1)
+
+    run_items([
+        Item(lambda t=t: answer_tile(t), [low(0), high(0)], wide(t % 2)) for t in range(4)
+    ], after_first)
+
+    for d1 in DISTANCES:
+        from_sibling(d1, -1)
+        from_sibling(d1, 1)
+
+    def after_second(n, top, acc):
+        keep(n, top, acc)
         if n == 1:
             arrived(own_keys(core, -1), R_A)
             pass_on(own_keys(core, -1, 0), R_A + 2, y_dev(1))
@@ -298,18 +302,18 @@
             pass_on(own_keys(core, 1, 1), R_A + 2, y_dev(-1))
             pass_on(own_keys(core, -1), R_ASIB + 1, sibling)
             pass_on(own_keys(core, 1), R_ASIB + 2, sibling)
-        if n == 2:
-            for d1 in DISTANCES:
-                arrived(shard(d1, 2), R_SECOND + 3 * DISTANCES.index(d1) + 2)
-                to_sibling(d1, 2)
-
-    run_items(first_items, after_first)
+        for d1 in ((), (), (0, -1), (1, 2))[n]:
+            hand_over(d1, 2)
+
+    run_items([
+        Item(lambda t=t: answer_tile(t), [f(d) for d in (-1, 1) for f in (low, high)],
+             wide(t % 2), lambda t=t: kept(t))
+        for t in range(4)
+    ], after_second)
 
     for d1 in DISTANCES:
         from_sibling(d1, 2)
     arrived(qp, R_QP)
-    arrived(own_keys(core, 2), R_A + 2)
-    pass_on(own_keys(core, 2), R_ASIB + 3, sibling)
 
     def prompt_mask(h):
         rows = iota(256, 0)
@@ -322,24 +326,24 @@
 
     prompt_order = (3, 2, 1, 0)
     answer_order = (2, 1, 3, 0)
-    second_items = []
+    last_items = []
     for t in prompt_order:
         pieces = [half_slab(i, h) for i in range(t) for h in range(2)]
         pieces += [half_slab(t, h, lambda h=h: prompt_mask(h)) for h in range(2)]
-        second_items.append(Item(lambda t=t: prompt_tile(t), pieces, tall(len(second_items) % 2)))
+        last_items.append(Item(lambda t=t: prompt_tile(t), pieces, tall(len(last_items) % 2)))
     for dx in answer_order:
         t = (x + dx) % 4
         own_piece = (
             lambda t=t: akv[0, t].reshape(512, DH), lambda t=t: akv[1, t].reshape(512, DH),
             answer_mask)
-        second_items.append(Item(
-            lambda t=t: answer_tile(t), [low(2), high(2), own_piece], wide(len(second_items) % 2),
-            lambda t=t: (tops[t][:, :1], accs[t])))
+        last_items.append(Item(
+            lambda t=t: answer_tile(t), [low(2), high(2), own_piece], wide(len(last_items) % 2),
+            lambda t=t: kept(t)))
 
     def finished(acc):
         return (acc[:, :DH] / acc[:, DH:]).astype(jnp.bfloat16)
 
-    def after_second(n, top, acc):
+    def after_last(n, top, acc):
         if n < 4:
             t = prompt_order[n]
             out = finished(acc)
@@ -359,6 +363,9 @@
                 @pl.when(g == me)
                 def _(g=g, dst=dst):
                     pltpu.make_async_copy(op.at[g], dst, recv_sems.at[R_OP]).start()
+            if n == 1:
+                arrived(own_keys(core, 2), R_A + 2)
+                pass_on(own_keys(core, 2), R_ASIB + 3, sibling)
             if n == 2:
                 for dy, r in ((0, 0), (-1, 1), (1, 2), (2, 3)):
                     arrived(own_keys(other, dy), R_ASIB + r)
@@ -379,7 +386,7 @@
             else:
                 pltpu.make_async_copy(oa.at[g], dst, recv_sems.at[R_OA]).start()
 
-    run_items(second_items, after_second)
+    run_items(last_items, after_last)
 
     assert len(sends) <= N_SEND
     for copy in sends:
@@ -399,6 +406,17 @@
         pltpu.make_async_copy(oa.at[i], oa.at[i], aout_sems.at[i]).wait()
     arrived(po, R_OP)
     arrived(ao, R_OA)
+
+
+def closing(lengths, prompt_in, answer_in, prompt_out, answer_out):
+    seq, resp = lax.axis_index("seq"), lax.axis_index("resp")
+    height = answer_in.shape[0]
+    live = lengths[seq // 2] - (seq % 2) * 256 - resp * height
+    prompt_out[...] = prompt_in[...]
+    for i in range(0, answer_in.shape[1], 1024):
+        rows = lax.broadcasted_iota(jnp.int32, (height, 1024), 0)
+        values = answer_in[:, i:i + 1024].astype(jnp.float32)
+        answer_out[:, i:i + 1024] = jnp.where(rows < live, values, 0.0).astype(jnp.bfloat16)
 
 
 def shards(pq, pk, pv, aq, ak, av, answer_lengths):
@@ -433,12 +451,17 @@
         cost_estimate=pl.CostEstimate(
             flops=6_400_000_000, bytes_accessed=2_000_000, transcendentals=12_000_000),
     )(pq, pk, pv, aq, ak, av)
-    seq, resp = lax.axis_index("seq"), lax.axis_index("resp")
-    height = aq.shape[0]
-    places = (seq % 2) * 256 + resp * height + jnp.arange(height, dtype=jnp.int32)
-    live = lax.dynamic_index_in_dim(answer_lengths, seq // 2, 0, keepdims=False)
-    answer_out = jnp.where((places < live)[:, None], answer_out, jnp.zeros((), bf16))
-    return prompt_out, answer_out
+    vmem = pl.BlockSpec(memory_space=pltpu.VMEM)
+    return pl.pallas_call(
+        closing,
+        out_shape=(
+            jax.ShapeDtypeStruct(pq.shape, bf16),
+            jax.ShapeDtypeStruct(aq.shape, bf16),
+        ),
+        in_specs=[pl.BlockSpec(memory_space=pltpu.SMEM), vmem, vmem],
+        out_specs=(vmem, vmem),
+        name="closing",
+    )(answer_lengths, prompt_out, answer_out)
 
 
 def solution(mesh):

time: 72.6 us -> 74.4 us (1.025)
  Pallas kernels: 67.2 us -> 73.7 us
  other arithmetic: 2.63 us -> 0 us
  local copies, waits for them, and re-layouts: 1.94 us -> 0 us
    pallas_call x1, Pallas kernels: 67.2 us -> 71.6 us  [shards(): pl.pallas_call(kernel, out_shape=(jax.ShapeDtypeStruct(pq.shape, bf16), j...]
    pallas_call x0 -> x1, Pallas kernels: none -> 2.04 us  [shards(): pl.pallas_call(closing, out_shape=(jax.ShapeDtypeStruct(pq.shape, bf16),...]
    select_n x1 -> x0, other arithmetic: 1.98 us -> none  [shards(): jnp.where((places < live)[:, None], answer_out, jnp.zeros((), bf16))]
    unnamed x5 -> x0, local copies, waits for them, and re-layouts: 1.35 us -> none
where the time goes in v4:
time: 74.4 us; the launch traced here: 74.3 us
  Pallas kernels  73.7 us (99%)
    pallas_call x1, Pallas kernels, shards(): pl.pallas_call(kernel, out_shape=(jax.ShapeDtypeStruct(pq.shape, bf16), j...  71.6 us
    pallas_call x1, Pallas kernels, shards(): pl.pallas_call(closing, out_shape=(jax.ShapeDtypeStruct(pq.shape, bf16),...  2.04 us

profile of v4, /device:TPU:1, one launch (start us, length us, event | category | flops | bytes accessed | tf_op | source)
XLA Modules:
  0.0 74.3 jit_solution(11733046713839593826)
XLA Ops:
  0.6 71.6 %shard_map.86 = (bf16[16,8192]{1,0:T(8,128)(2,1)}, bf16[32,8192]{1,0:T(8,128)(2,1)}) custom-call(bf16[16,8192]{1,0:T(8,128)(2,1)} %pq.1, bf16[16,1024]{1,0:T(8,128)(2,1)} %pk.1, bf16[16,1024]{1,0:T(8,128)(2,1)} %pv.1, bf16[32,8192]{1,0:T(8,128)(2,1)} %aq.1, bf16[32,1024]{1,0:T(8,128)(2,1)} %ak.1, bf16[32,1024]{1,0:T(8,128)(2,1)} %av.1), custom_call_target="tpu_custom_call" | custom-call | flops 6400000000 | bytes 2000000 | tf_op jit(solution)/shard_map/pallas_call | solution.py:425
  72.3 2.0 %closing.1 = (bf16[16,8192]{1,0:T(8,128)(2,1)}, bf16[32,8192]{1,0:T(8,128)(2,1)}) custom-call(s32[16]{0:T(128)} %lengths.1, bf16[16,8192]{1,0:T(8,128)(2,1)} %get-tuple-element.4.prompt_in, bf16[32,8192]{1,0:T(8,128)(2,1)} %get-tuple-element.5.answer_in), custom_call_target="tpu_custom_call" | custom-call | tf_op jit(solution)/shard_map/closing/pallas_call | solution.py:455

commit v5 on v4

--- a/solution.py
+++ b/solution.py
@@ -120,7 +120,7 @@
         (h * 2 + (core + dc) % 2, place(xx, zz, y, (core + dc) % 2))
         for h, xx, zz in chips for dc in range(2)
     ]
-    partners = [dev for _, dev in members[1:]] + [f(d) for f in (first, second) for d in (1, -1, 2)]
+    partners = [dev for _, dev in members[1:]] + [first(1), first(-1), first(2), second(1), second(-1)]
 
     barrier = pltpu.get_barrier_semaphore()
     for dev in partners:
@@ -190,13 +190,24 @@
 
     def start_second(d1):
         r = R_SECOND + 3 * DISTANCES.index(d1)
-        for k, d in enumerate((1, -1, 2)):
-            pass_on(shard(d1, 0), r + k, second(d))
-
-    def hand_over(d1, d2):
-        k = DISTANCES[1:].index(d2)
-        arrived(shard(d1, d2), R_SECOND + 3 * DISTANCES.index(d1) + k)
-        to_sibling(d1, d2)
+        pass_on(shard(d1, 0), r, second(1))
+        pass_on(shard(d1, 0), r + 1, second(-1))
+
+    def middle_second(d1):
+        r = R_SECOND + 3 * DISTANCES.index(d1)
+        arrived(shard(d1, -1), r)
+        pass_on(part_of(core, d1, -1, 0), r + 2, second(1))
+        arrived(shard(d1, 1), r + 1)
+        pass_on(part_of(core, d1, 1, 1), r + 2, second(-1))
+        to_sibling(d1, -1)
+        to_sibling(d1, 1)
+
+    def hand_over(d1):
+        arrived(shard(d1, 2), R_SECOND + 3 * DISTANCES.index(d1) + 2)
+        to_sibling(d1, 2)
+
+    def own_keys(c, dy, n=slice(None)):
+        return akv.at[n, pl.ds(2 * c, 2), :, around(y, dy)]
 
     for d in (7, 6, 5, 4, 3, 2, 1):
         h, xx, zz = chips[d]
@@ -222,11 +233,14 @@
         h, xx, zz = chips[d]
         send(cut(ak, h, DH), ak_land, R_AKV, place(xx, zz, y, mine))
         send(cut(av, h, DH), av_land, R_AKV, place(xx, zz, y, mine))
+    for d1 in DISTANCES:
+        middle_second(d1)
+    arrived(own_keys(core, 0), R_AKV)
+    pass_on(own_keys(core, 0), R_A, y_dev(1))
+    pass_on(own_keys(core, 0), R_A + 1, y_dev(-1))
+    pass_on(own_keys(core, 0), R_ASIB, sibling)
     for g, dev in members[:0:-1]:
         send(cut(pq, g, QW), qp.at[me], R_QP, dev)
-
-    def own_keys(c, dy, n=slice(None)):
-        return akv.at[n, pl.ds(2 * c, 2), :, around(y, dy)]
 
     bufs = (s0, s1)
 
@@ -269,47 +283,29 @@
     def kept(t):
         return tops[t][:, :1], accs[t]
 
-    for d1 in DISTANCES:
-        from_sibling(d1, 0)
+    for d2 in (0, -1, 1):
+        for d1 in DISTANCES:
+            from_sibling(d1, d2)
     arrived(qa, R_QA)
 
     def after_first(n, top, acc):
         keep(n, top, acc)
-        if n == 0:
-            arrived(own_keys(core, 0), R_AKV)
-            pass_on(own_keys(core, 0), R_A, y_dev(1))
-            pass_on(own_keys(core, 0), R_A + 1, y_dev(-1))
-            pass_on(own_keys(core, 0), R_ASIB, sibling)
-        else:
-            for d1 in ((), (0,), (-1, 1), (2,))[n]:
-                hand_over(d1, -1)
-                hand_over(d1, 1)
-
-    run_items([
-        Item(lambda t=t: answer_tile(t), [low(0), high(0)], wide(t % 2)) for t in range(4)
-    ], after_first)
-
-    for d1 in DISTANCES:
-        from_sibling(d1, -1)
-        from_sibling(d1, 1)
-
-    def after_second(n, top, acc):
-        keep(n, top, acc)
         if n == 1:
+            for d1 in DISTANCES:
+                hand_over(d1)
+        if n == 2:
             arrived(own_keys(core, -1), R_A)
             pass_on(own_keys(core, -1, 0), R_A + 2, y_dev(1))
             arrived(own_keys(core, 1), R_A + 1)
             pass_on(own_keys(core, 1, 1), R_A + 2, y_dev(-1))
             pass_on(own_keys(core, -1), R_ASIB + 1, sibling)
             pass_on(own_keys(core, 1), R_ASIB + 2, sibling)
-        for d1 in ((), (), (0, -1), (1, 2))[n]:
-            hand_over(d1, 2)
 
     run_items([
-        Item(lambda t=t: answer_tile(t), [f(d) for d in (-1, 1) for f in (low, high)],
-             wide(t % 2), lambda t=t: kept(t))
+        Item(lambda t=t: answer_tile(t),
+             [f(d) for d in (0, -1, 1) for f in (low, high)], wide(t % 2))
         for t in range(4)
-    ], after_second)
+    ], after_first)
 
     for d1 in DISTANCES:
         from_sibling(d1, 2)

time: 74.4 us -> 68 us (0.914)
  Pallas kernels: 73.7 us -> 67.2 us
    pallas_call x1, Pallas kernels: 71.6 us -> 65.2 us  [shards(): pl.pallas_call(kernel, out_shape=(jax.ShapeDtypeStruct(pq.shape, bf16), j...]
where the time goes in v5:
time: 68 us; the launch traced here: 67.9 us
  Pallas kernels  67.2 us (99%)
    pallas_call x1, Pallas kernels, shards(): pl.pallas_call(kernel, out_shape=(jax.ShapeDtypeStruct(pq.shape, bf16), j...  65.2 us
    pallas_call x1, Pallas kernels, shards(): pl.pallas_call(closing, out_shape=(jax.ShapeDtypeStruct(pq.shape, bf16),...  2.04 us

profile of v5, /device:TPU:1, one launch (start us, length us, event | category | flops | bytes accessed | tf_op | source)
XLA Modules:
  0.0 67.9 jit_solution(10308155477615842234)
XLA Ops:
  0.6 65.2 %shard_map.86 = (bf16[16,8192]{1,0:T(8,128)(2,1)}, bf16[32,8192]{1,0:T(8,128)(2,1)}) custom-call(bf16[16,8192]{1,0:T(8,128)(2,1)} %pq.1, bf16[16,1024]{1,0:T(8,128)(2,1)} %pk.1, bf16[16,1024]{1,0:T(8,128)(2,1)} %pv.1, bf16[32,8192]{1,0:T(8,128)(2,1)} %aq.1, bf16[32,1024]{1,0:T(8,128)(2,1)} %ak.1, bf16[32,1024]{1,0:T(8,128)(2,1)} %av.1), custom_call_target="tpu_custom_call" | custom-call | flops 6400000000 | bytes 2000000 | tf_op jit(solution)/shard_map/pallas_call | solution.py:421
  65.9 2.0 %closing.1 = (bf16[16,8192]{1,0:T(8,128)(2,1)}, bf16[32,8192]{1,0:T(8,128)(2,1)}) custom-call(s32[16]{0:T(128)} %lengths.1, bf16[16,8192]{1,0:T(8,128)(2,1)} %get-tuple-element.4.prompt_in, bf16[32,8192]{1,0:T(8,128)(2,1)} %get-tuple-element.5.answer_in), custom_call_target="tpu_custom_call" | custom-call | tf_op jit(solution)/shard_map/closing/pallas_call | solution.py:451

commit v6 on v5

--- a/solution.py
+++ b/solution.py
@@ -165,7 +165,7 @@
     def arrived(ref, r):
         pltpu.make_async_copy(ref, ref, recv_sems.at[r]).wait()
 
-    own_sends = [remote(src, dst, aout_sems.at[16 + i], r, sibling)
+    own_sends = [remote(src, dst, aout_sems.at[1 + i], r, sibling)
                  for i, (src, dst, r) in enumerate(own_parts)]
 
     def part_of(c, d1, d2, n=slice(None)):
@@ -219,26 +219,24 @@
         for copy in own_sends:
             copy.start()
 
+    for d in (7, 6, 5, 4, 3, 2, 1):
+        h, xx, zz = chips[d]
+        send(cut(ak, h, DH), ak_land, R_AKV, place(xx, zz, y, mine))
+        send(cut(av, h, DH), av_land, R_AKV, place(xx, zz, y, mine))
     arrived(shard(0, 0), R_KV)
     start_first()
     start_second(0)
     to_sibling(0, 0)
+    arrived(own_keys(core, 0), R_AKV)
+    pass_on(own_keys(core, 0), R_A, y_dev(1))
+    pass_on(own_keys(core, 0), R_A + 1, y_dev(-1))
+    pass_on(own_keys(core, 0), R_ASIB, sibling)
     for g, dev in members[:0:-1]:
         send(cut(aq, g, QW), qa.at[me], R_QA, dev)
     for k, d1 in enumerate((-1, 1, 2)):
         arrived(shard(d1, 0), R_FIRST + k)
         start_second(d1)
         to_sibling(d1, 0)
-    for d in (7, 6, 5, 4, 3, 2, 1):
-        h, xx, zz = chips[d]
-        send(cut(ak, h, DH), ak_land, R_AKV, place(xx, zz, y, mine))
-        send(cut(av, h, DH), av_land, R_AKV, place(xx, zz, y, mine))
-    for d1 in DISTANCES:
-        middle_second(d1)
-    arrived(own_keys(core, 0), R_AKV)
-    pass_on(own_keys(core, 0), R_A, y_dev(1))
-    pass_on(own_keys(core, 0), R_A + 1, y_dev(-1))
-    pass_on(own_keys(core, 0), R_ASIB, sibling)
     for g, dev in members[:0:-1]:
         send(cut(pq, g, QW), qp.at[me], R_QP, dev)
 
@@ -283,33 +281,48 @@
     def kept(t):
         return tops[t][:, :1], accs[t]
 
-    for d2 in (0, -1, 1):
+    early = len(sends)
+
+    for d1 in DISTANCES:
+        from_sibling(d1, 0)
+    arrived(qa, R_QA)
+    run_items([
+        Item(lambda t=t: answer_tile(t), [low(0), high(0)], wide(t % 2)) for t in range(4)
+    ], keep)
+
+    for d1 in DISTANCES:
+        middle_second(d1)
+    arrived(own_keys(core, -1), R_A)
+    pass_on(own_keys(core, -1, 0), R_A + 2, y_dev(1))
+    arrived(own_keys(core, 1), R_A + 1)
+    pass_on(own_keys(core, 1, 1), R_A + 2, y_dev(-1))
+    pass_on(own_keys(core, -1), R_ASIB + 1, sibling)
+    pass_on(own_keys(core, 1), R_ASIB + 2, sibling)
+    for copy in sends[:early]:
+        copy.wait_send()
+    for d2 in (-1, 1):
         for d1 in DISTANCES:
             from_sibling(d1, d2)
-    arrived(qa, R_QA)
-
-    def after_first(n, top, acc):
+
+    def after_second(n, top, acc):
         keep(n, top, acc)
-        if n == 1:
+        if n == 2:
             for d1 in DISTANCES:
                 hand_over(d1)
-        if n == 2:
-            arrived(own_keys(core, -1), R_A)
-            pass_on(own_keys(core, -1, 0), R_A + 2, y_dev(1))
-            arrived(own_keys(core, 1), R_A + 1)
-            pass_on(own_keys(core, 1, 1), R_A + 2, y_dev(-1))
-            pass_on(own_keys(core, -1), R_ASIB + 1, sibling)
-            pass_on(own_keys(core, 1), R_ASIB + 2, sibling)
+            arrived(own_keys(core, 2), R_A + 2)
+            pass_on(own_keys(core, 2), R_ASIB + 3, sibling)
 
     run_items([
-        Item(lambda t=t: answer_tile(t),
-             [f(d) for d in (0, -1, 1) for f in (low, high)], wide(t % 2))
+        Item(lambda t=t: answer_tile(t), [f(d) for d in (-1, 1) for f in (low, high)],
+             wide(t % 2), lambda t=t: kept(t))
         for t in range(4)
-    ], after_first)
+    ], after_second)
 
     for d1 in DISTANCES:
         from_sibling(d1, 2)
     arrived(qp, R_QP)
+    for dy, r in ((0, 0), (-1, 1), (1, 2), (2, 3)):
+        arrived(own_keys(other, dy), R_ASIB + r)
 
     def prompt_mask(h):
         rows = iota(256, 0)
@@ -323,10 +336,6 @@
     prompt_order = (3, 2, 1, 0)
     answer_order = (2, 1, 3, 0)
     last_items = []
-    for t in prompt_order:
-        pieces = [half_slab(i, h) for i in range(t) for h in range(2)]
-        pieces += [half_slab(t, h, lambda h=h: prompt_mask(h)) for h in range(2)]
-        last_items.append(Item(lambda t=t: prompt_tile(t), pieces, tall(len(last_items) % 2)))
     for dx in answer_order:
         t = (x + dx) % 4
         own_piece = (
@@ -335,13 +344,17 @@
         last_items.append(Item(
             lambda t=t: answer_tile(t), [low(2), high(2), own_piece], wide(len(last_items) % 2),
             lambda t=t: kept(t)))
+    for t in prompt_order:
+        pieces = [half_slab(i, h) for i in range(t) for h in range(2)]
+        pieces += [half_slab(t, h, lambda h=h: prompt_mask(h)) for h in range(2)]
+        last_items.append(Item(lambda t=t: prompt_tile(t), pieces, tall(len(last_items) % 2)))
 
     def finished(acc):
         return (acc[:, :DH] / acc[:, DH:]).astype(jnp.bfloat16)
 
     def after_last(n, top, acc):
-        if n < 4:
-            t = prompt_order[n]
+        if n >= 4:
+            t = prompt_order[n - 4]
             out = finished(acc)
             for j in range(4):
                 for c in range(4):
@@ -353,20 +366,14 @@
 
                 @pl.when(g != me)
                 def _(g=g, c=c, dst=dst):
-                    remote(op.at[g], dst, pout_sems.at[g], R_OP,
+                    remote(op.at[g], dst, pout_sems.at[0], R_OP,
                            place(t, zh * 2 + c // 2, y, c % 2)).start()
 
                 @pl.when(g == me)
                 def _(g=g, dst=dst):
                     pltpu.make_async_copy(op.at[g], dst, recv_sems.at[R_OP]).start()
-            if n == 1:
-                arrived(own_keys(core, 2), R_A + 2)
-                pass_on(own_keys(core, 2), R_ASIB + 3, sibling)
-            if n == 2:
-                for dy, r in ((0, 0), (-1, 1), (1, 2), (2, 3)):
-                    arrived(own_keys(other, dy), R_ASIB + r)
             return
-        dx = answer_order[n - 4]
+        dx = answer_order[n]
         t = (x + dx) % 4
         out = finished(acc)
         for j in range(4):
@@ -378,14 +385,14 @@
             d = dx * 4 + k
             g, dev = members[d]
             if d:
-                remote(oa.at[g], dst, aout_sems.at[d], R_OA, dev).start()
+                remote(oa.at[g], dst, aout_sems.at[0], R_OA, dev).start()
             else:
                 pltpu.make_async_copy(oa.at[g], dst, recv_sems.at[R_OA]).start()
 
     run_items(last_items, after_last)
 
     assert len(sends) <= N_SEND
-    for copy in sends:
+    for copy in sends[early:]:
         copy.wait_send()
 
     @pl.when(core != mine)
@@ -393,13 +400,8 @@
         for copy in own_sends:
             copy.wait_send()
 
-    for g in range(16):
-        @pl.when(g != me)
-        def _(g=g):
-            pltpu.make_async_copy(op.at[g], op.at[g], pout_sems.at[g]).wait()
-
-    for i in range(1, 16):
-        pltpu.make_async_copy(oa.at[i], oa.at[i], aout_sems.at[i]).wait()
+    pltpu.make_async_copy(op.at[0:15], op.at[0:15], pout_sems.at[0]).wait()
+    pltpu.make_async_copy(oa.at[0:15], oa.at[0:15], aout_sems.at[0]).wait()
     arrived(po, R_OP)
     arrived(ao, R_OA)
 
@@ -438,8 +440,8 @@
             pltpu.VMEM((6, 512, 512), f32),
             pltpu.VMEM((6, 512, 512), f32),
             pltpu.SemaphoreType.DMA((N_SEND,)),
-            pltpu.SemaphoreType.DMA((16,)),
-            pltpu.SemaphoreType.DMA((20,)),
+            pltpu.SemaphoreType.DMA((1,)),
+            pltpu.SemaphoreType.DMA((5,)),
             pltpu.SemaphoreType.DMA((N_RECV,)),
         ],
         compiler_params=pltpu.CompilerParams(

time: 68 us -> 64.6 us (0.950)
  Pallas kernels: 67.2 us -> 63.8 us
    pallas_call x1, Pallas kernels: 65.2 us -> 61.8 us  [shards(): pl.pallas_call(kernel, out_shape=(jax.ShapeDtypeStruct(pq.shape, bf16), j...]
where the time goes in v6:
time: 64.6 us; the launch traced here: 64.5 us
  Pallas kernels  63.8 us (99%)
    pallas_call x1, Pallas kernels, shards(): pl.pallas_call(kernel, out_shape=(jax.ShapeDtypeStruct(pq.shape, bf16), j...  61.8 us
    pallas_call x1, Pallas kernels, shards(): pl.pallas_call(closing, out_shape=(jax.ShapeDtypeStruct(pq.shape, bf16),...  2.04 us

profile of v6, /device:TPU:1, one launch (start us, length us, event | category | flops | bytes accessed | tf_op | source)
XLA Modules:
  0.0 64.5 jit_solution(8511383223457468330)
XLA Ops:
  0.6 61.8 %shard_map.86 = (bf16[16,8192]{1,0:T(8,128)(2,1)}, bf16[32,8192]{1,0:T(8,128)(2,1)}) custom-call(bf16[16,8192]{1,0:T(8,128)(2,1)} %pq.1, bf16[16,1024]{1,0:T(8,128)(2,1)} %pk.1, bf16[16,1024]{1,0:T(8,128)(2,1)} %pv.1, bf16[32,8192]{1,0:T(8,128)(2,1)} %aq.1, bf16[32,1024]{1,0:T(8,128)(2,1)} %ak.1, bf16[32,1024]{1,0:T(8,128)(2,1)} %av.1), custom_call_target="tpu_custom_call" | custom-call | flops 6400000000 | bytes 2000000 | tf_op jit(solution)/shard_map/pallas_call | solution.py:423
  62.4 2.0 %closing.1 = (bf16[16,8192]{1,0:T(8,128)(2,1)}, bf16[32,8192]{1,0:T(8,128)(2,1)}) custom-call(s32[16]{0:T(128)} %lengths.1, bf16[16,8192]{1,0:T(8,128)(2,1)} %get-tuple-element.4.prompt_in, bf16[32,8192]{1,0:T(8,128)(2,1)} %get-tuple-element.5.answer_in), custom_call_target="tpu_custom_call" | custom-call | tf_op jit(solution)/shard_map/closing/pallas_call | solution.py:453

commit v7 on v6

--- a/solution.py
+++ b/solution.py
@@ -237,8 +237,6 @@
         arrived(shard(d1, 0), R_FIRST + k)
         start_second(d1)
         to_sibling(d1, 0)
-    for g, dev in members[:0:-1]:
-        send(cut(pq, g, QW), qp.at[me], R_QP, dev)
 
     bufs = (s0, s1)
 
@@ -298,6 +296,8 @@
     pass_on(own_keys(core, 1, 1), R_A + 2, y_dev(-1))
     pass_on(own_keys(core, -1), R_ASIB + 1, sibling)
     pass_on(own_keys(core, 1), R_ASIB + 2, sibling)
+    for g, dev in members[:0:-1]:
+        send(cut(pq, g, QW), qp.at[me], R_QP, dev)
     for copy in sends[:early]:
         copy.wait_send()
     for d2 in (-1, 1):
@@ -320,7 +320,6 @@
 
     for d1 in DISTANCES:
         from_sibling(d1, 2)
-    arrived(qp, R_QP)
     for dy, r in ((0, 0), (-1, 1), (1, 2), (2, 3)):
         arrived(own_keys(other, dy), R_ASIB + r)
 
@@ -353,6 +352,8 @@
         return (acc[:, :DH] / acc[:, DH:]).astype(jnp.bfloat16)
 
     def after_last(n, top, acc):
+        if n == 2:
+            arrived(qp, R_QP)
         if n >= 4:
             t = prompt_order[n - 4]
             out = finished(acc)

time: 64.6 us -> 64.9 us (level)
  no operation moved by 1% of the time
where the time goes in v7:
time: 64.9 us; the launch traced here: 64.7 us
  Pallas kernels  64.1 us (99%)
    pallas_call x1, Pallas kernels, shards(): pl.pallas_call(kernel, out_shape=(jax.ShapeDtypeStruct(pq.shape, bf16), j...  62.1 us
    pallas_call x1, Pallas kernels, shards(): pl.pallas_call(closing, out_shape=(jax.ShapeDtypeStruct(pq.shape, bf16),...  2.04 us

profile of v7, /device:TPU:1, one launch (start us, length us, event | category | flops | bytes accessed | tf_op | source)
XLA Modules:
  0.0 64.7 jit_solution(12825642945640301830)
XLA Ops:
  0.6 62.1 %shard_map.86 = (bf16[16,8192]{1,0:T(8,128)(2,1)}, bf16[32,8192]{1,0:T(8,128)(2,1)}) custom-call(bf16[16,8192]{1,0:T(8,128)(2,1)} %pq.1, bf16[16,1024]{1,0:T(8,128)(2,1)} %pk.1, bf16[16,1024]{1,0:T(8,128)(2,1)} %pv.1, bf16[32,8192]{1,0:T(8,128)(2,1)} %aq.1, bf16[32,1024]{1,0:T(8,128)(2,1)} %ak.1, bf16[32,1024]{1,0:T(8,128)(2,1)} %av.1), custom_call_target="tpu_custom_call" | custom-call | flops 6400000000 | bytes 2000000 | tf_op jit(solution)/shard_map/pallas_call | solution.py:424
  62.7 2.0 %closing.1 = (bf16[16,8192]{1,0:T(8,128)(2,1)}, bf16[32,8192]{1,0:T(8,128)(2,1)}) custom-call(s32[16]{0:T(128)} %lengths.1, bf16[16,8192]{1,0:T(8,128)(2,1)} %get-tuple-element.4.prompt_in, bf16[32,8192]{1,0:T(8,128)(2,1)} %get-tuple-element.5.answer_in), custom_call_target="tpu_custom_call" | custom-call | tf_op jit(solution)/shard_map/closing/pallas_call | solution.py:454

commit v8 on v6

--- a/solution.py
+++ b/solution.py
@@ -342,19 +342,21 @@
             lambda t=t: akv[0, t].reshape(512, DH), lambda t=t: akv[1, t].reshape(512, DH),
             answer_mask)
         last_items.append(Item(
-            lambda t=t: answer_tile(t), [low(2), high(2), own_piece], wide(len(last_items) % 2),
+            lambda t=t: answer_tile(t), [low(2), high(2), own_piece], wide((0, 1, 0, 1)[len(last_items)]),
             lambda t=t: kept(t)))
     for t in prompt_order:
         pieces = [half_slab(i, h) for i in range(t) for h in range(2)]
         pieces += [half_slab(t, h, lambda h=h: prompt_mask(h)) for h in range(2)]
-        last_items.append(Item(lambda t=t: prompt_tile(t), pieces, tall(len(last_items) % 2)))
+        last_items.append(Item(lambda t=t: prompt_tile(t), pieces, tall((len(last_items) + 1) % 2)))
+
+    last_items.append(last_items.pop(3))
 
     def finished(acc):
         return (acc[:, :DH] / acc[:, DH:]).astype(jnp.bfloat16)
 
     def after_last(n, top, acc):
-        if n >= 4:
-            t = prompt_order[n - 4]
+        if 3 <= n < 7:
+            t = prompt_order[n - 3]
             out = finished(acc)
             for j in range(4):
                 for c in range(4):
@@ -373,7 +375,7 @@
                 def _(g=g, dst=dst):
                     pltpu.make_async_copy(op.at[g], dst, recv_sems.at[R_OP]).start()
             return
-        dx = answer_order[n]
+        dx = answer_order[min(n, 3)]
         t = (x + dx) % 4
         out = finished(acc)
         for j in range(4):

time: 64.6 us -> 64.1 us (level)
  no operation moved by 1% of the time
where the time goes in v8:
time: 64.1 us; the launch traced here: 64 us
  Pallas kernels  63.4 us (99%)
    pallas_call x1, Pallas kernels, shards(): pl.pallas_call(kernel, out_shape=(jax.ShapeDtypeStruct(pq.shape, bf16), j...  61.3 us
    pallas_call x1, Pallas kernels, shards(): pl.pallas_call(closing, out_shape=(jax.ShapeDtypeStruct(pq.shape, bf16),...  2.04 us

profile of v8, /device:TPU:1, one launch (start us, length us, event | category | flops | bytes accessed | tf_op | source)
XLA Modules:
  0.0 64.0 jit_solution(3764416861164862222)
XLA Ops:
  0.6 61.3 %shard_map.86 = (bf16[16,8192]{1,0:T(8,128)(2,1)}, bf16[32,8192]{1,0:T(8,128)(2,1)}) custom-call(bf16[16,8192]{1,0:T(8,128)(2,1)} %pq.1, bf16[16,1024]{1,0:T(8,128)(2,1)} %pk.1, bf16[16,1024]{1,0:T(8,128)(2,1)} %pv.1, bf16[32,8192]{1,0:T(8,128)(2,1)} %aq.1, bf16[32,1024]{1,0:T(8,128)(2,1)} %ak.1, bf16[32,1024]{1,0:T(8,128)(2,1)} %av.1), custom_call_target="tpu_custom_call" | custom-call | flops 6400000000 | bytes 2000000 | tf_op jit(solution)/shard_map/pallas_call | solution.py:425
  62.0 2.0 %closing.1 = (bf16[16,8192]{1,0:T(8,128)(2,1)}, bf16[32,8192]{1,0:T(8,128)(2,1)}) custom-call(s32[16]{0:T(128)} %lengths.1, bf16[16,8192]{1,0:T(8,128)(2,1)} %get-tuple-element.4.prompt_in, bf16[32,8192]{1,0:T(8,128)(2,1)} %get-tuple-element.5.answer_in), custom_call_target="tpu_custom_call" | custom-call | tf_op jit(solution)/shard_map/closing/pallas_call | solution.py:455
